TPU v7x, 32 devices: a whole 2x2x4 slice. The times are simulated.
32 devices in a mesh: dp: 4 (over z), pipe: 4 (over y, x), seq: 2 (over core).
Axes of the slice: x: 2, y: 2, z: 4, core: 2. Of those that a mesh axis runs over, the one named last changes fastest.
Arguments:
- section_input: bfloat16 [4, 4, 256, 1024], P('pipe', 'dp', 'seq'), may hold values from -6 to 6
- event_ids: int32 [4, 256], P('dp', 'seq'), may hold values from 0 to 63
- lengths: int32 [4], P('dp'), may hold values from 64 to 256, as said below
- clicks: int32 [4, 256], P('dp', 'seq'), may hold values 0 or 1
- conversions: int32 [4, 256], P('dp', 'seq'), may hold values 0 or 1
- conv_weight: bfloat16 [4, 3072, 1024], P('pipe'), may hold values from -0.109375 to 0.109375
- type_table: bfloat16 [4, 64, 1024], P('pipe'), may hold values from -3 to 3
- head_weight: bfloat16 [2, 1024], replicated, may hold values from -0.375 to 0.375
Outputs:
- conv_grad: float32 [4, 3072, 1024], P('pipe', ('dp', 'seq'))
- type_grad: float32 [4, 64, 1024], P('pipe', ('dp', 'seq'))
- input_grad: bfloat16 [4, 4, 256, 1024], P('pipe', 'dp', 'seq')
Inputs may be any that keep to these rules, and one draw needn't show every extreme that they name: `lengths`: some history has all 256 events real.
All inputs are finite; a program needn't handle non-finite values. No bound on the sum of `clicks` or of `conversions` on one device may be relied on, other than what follows from the above.
Results may differ from a plain program's by a relative error of at most 0.013.
Values may be sent and summed in bfloat16 or wider, within the bound.
A program may use at most 256 MiB of HBM per device.

v0:
```python
import jax
import jax.numpy as jnp
from jax import lax
from jax.sharding import PartitionSpec as P

KERNEL = 3


EPS = 1e-06


def from_behind(array, axis, by):
    count = lax.axis_size(axis)
    pairs = [(i, i + by) for i in range(count) if 0 <= i + by < count]
    return lax.ppermute(array, axis, pairs)


def head_grad(out_bf, head_weight, click, convert, valid):
    logits = jnp.dot(out_bf, head_weight.T, preferred_element_type=jnp.float32)
    label_y = click.astype(jnp.float32)
    label_z = label_y * convert.astype(jnp.float32)
    weight_m = valid.astype(jnp.float32)

    def event_loss(first, second):
        soft = jax.nn.softplus
        rest = jnp.log(jax.nn.sigmoid(-first) + jax.nn.sigmoid(first) * jax.nn.sigmoid(-second))
        return (
            label_y * soft(-first)
            + (1.0 - label_y) * soft(first)
            + label_z * (soft(-first) + soft(-second))
            - (1.0 - label_z) * rest
        )

    _, pull = jax.vjp(event_loss, logits[:, 0], logits[:, 1])
    grad_first, grad_second = pull(weight_m)
    grad_logits = jnp.stack([grad_first, grad_second], axis=1)
    return jnp.dot(grad_logits, head_weight.astype(jnp.float32), precision=lax.Precision.HIGHEST)


def on_device(
    section_input, event_ids, lengths, clicks, conversions, conv_weight, type_table, head_weight
):
    inputs_bf = section_input[0, 0]
    rows, width = inputs_bf.shape
    halo_rows = rows // 2
    weight = conv_weight[0]
    table = type_table[0]
    kinds = table.shape[0]
    section = lax.axis_index("pipe")
    sections = lax.axis_size("pipe")
    spacing = jnp.right_shift(jnp.int32(rows // 4), section)
    inputs = inputs_bf.astype(jnp.float32)
    inv_rms = lax.rsqrt(jnp.mean(inputs * inputs, axis=-1, keepdims=True) + EPS)
    normed = inputs * inv_rms
    normed_bf = normed.astype(jnp.bfloat16)
    earlier = from_behind(normed_bf[rows - halo_rows :], "seq", 1)
    extended = jnp.concatenate([earlier, normed_bf], axis=0)
    taps = jnp.concatenate(
        [
            lax.dynamic_slice_in_dim(extended, halo_rows - tap * spacing, rows, 0)
            for tap in range(KERNEL)
        ],
        axis=1,
    )
    onehot = (event_ids[0][:, None] == jnp.arange(kinds, dtype=jnp.int32)[None, :]).astype(
        jnp.bfloat16
    )
    position = lax.axis_index("seq") * rows + jnp.arange(rows, dtype=jnp.int32)
    valid = position < lengths[0]
    is_last = section == sections - 1

    def forward_and_head():
        pre = jnp.dot(taps, weight, preferred_element_type=jnp.float32) + jnp.dot(
            onehot, table, preferred_element_type=jnp.float32
        )
        out_bf = (inputs + jax.nn.gelu(pre)).astype(jnp.bfloat16)
        return (pre, head_grad(out_bf, head_weight, clicks[0], conversions[0], valid))

    def active_work(incoming):
        pre, top_grad = forward_and_head()
        grad_out = jnp.where(is_last, top_grad, incoming)
        _, pull = jax.vjp(jax.nn.gelu, pre)
        grad_pre = pull(grad_out)[0].astype(jnp.bfloat16)
        conv_part = lax.dot_general(
            taps, grad_pre, (((0,), (0,)), ((), ())), preferred_element_type=jnp.float32
        )
        type_part = lax.dot_general(
            onehot, grad_pre, (((0,), (0,)), ((), ())), preferred_element_type=jnp.float32
        )
        grad_taps = lax.dot_general(
            grad_pre, weight, (((1,), (1,)), ((), ())), preferred_element_type=jnp.float32
        )
        grad_ext = jnp.zeros((halo_rows + rows, width), jnp.float32)
        for tap in range(KERNEL):
            start = halo_rows - tap * spacing
            current = lax.dynamic_slice_in_dim(grad_ext, start, rows, 0)
            grad_ext = lax.dynamic_update_slice_in_dim(
                grad_ext, current + grad_taps[:, tap * width : (tap + 1) * width], start, 0
            )
        return (conv_part, type_part, grad_ext, grad_out)

    def spare_work(incoming):
        return (
            jnp.zeros((KERNEL * width, width), jnp.float32),
            jnp.zeros((kinds, width), jnp.float32),
            jnp.zeros((halo_rows + rows, width), jnp.float32),
            jnp.zeros((rows, width), jnp.float32),
        )

    incoming = jnp.zeros((rows, width), jnp.float32)
    input_grad = jnp.zeros((rows, width), jnp.bfloat16)
    conv_total = jnp.zeros((KERNEL * width, width), jnp.float32)
    type_total = jnp.zeros((kinds, width), jnp.float32)
    for tick in range(sections):
        active = section == sections - 1 - tick
        reach = 2 * (rows // 4 >> sections - 1 - tick)
        conv_part, type_part, grad_ext, grad_out = lax.cond(
            active, active_work, spare_work, incoming
        )
        later = from_behind(
            grad_ext[halo_rows - reach : halo_rows].astype(jnp.bfloat16), "seq", -1
        ).astype(jnp.float32)
        grad_normed = grad_ext[halo_rows:] + jnp.concatenate(
            [jnp.zeros((rows - reach, width), jnp.float32), later], axis=0
        )
        inner = jnp.mean(grad_normed * normed, axis=-1, keepdims=True)
        grad_in = (grad_out + inv_rms * (grad_normed - normed * inner)).astype(jnp.bfloat16)
        input_grad = jnp.where(active, grad_in, input_grad)
        conv_total = conv_total + conv_part
        type_total = type_total + type_part
        if tick + 1 < sections:
            incoming = from_behind(grad_in, "pipe", -1).astype(jnp.float32)
    conv_mid, type_mid = (
        lax.psum_scatter(
            conv_total.astype(jnp.bfloat16), "dp", scatter_dimension=0, tiled=True
        ).astype(jnp.float32),
        lax.psum_scatter(
            type_total.astype(jnp.bfloat16), "dp", scatter_dimension=0, tiled=True
        ).astype(jnp.float32),
    )
    conv_share, type_share = (
        lax.psum_scatter(
            conv_mid.astype(jnp.bfloat16), "seq", scatter_dimension=0, tiled=True
        ).astype(jnp.float32),
        lax.psum_scatter(
            type_mid.astype(jnp.bfloat16), "seq", scatter_dimension=0, tiled=True
        ).astype(jnp.float32),
    )
    return (conv_share[None], type_share[None], input_grad[None, None])


def solution(mesh):
    placed = (
        P("pipe", "dp", "seq", None),
        P("dp", "seq"),
        P("dp"),
        P("dp", "seq"),
        P("dp", "seq"),
        P("pipe", None, None),
        P("pipe", None, None),
        P(),
    )
    return jax.shard_map(
        on_device,
        mesh=mesh,
        in_specs=placed,
        out_specs=(
            P("pipe", ("dp", "seq"), None),
            P("pipe", ("dp", "seq"), None),
            P("pipe", "dp", "seq", None),
        ),
        check_vma=False,
    )
```

profile of v0, /device:TPU:0, one launch (start us, length us, event | category | flops | bytes accessed | tf_op | source)
XLA Modules:
  0.0 374.7 jit_solution(11303226336769174886)
XLA Ops:
  9.4 2.4 collective-permute-start
  14.7 7.2 %conditional.4 = (f32[64,1024]{1,0:T(8,128)S(1)}, f32[192,1024]{1,0:T(8,128)}, f32[128,1024]{1,0:T(8,128)S(1)}, f32[3072,1024]{1,0:T(8,128)}) conditional(s32[]{:T(128)} %convert_element_type.153, () %tuple.40, (pred[]{:T(512)}, s32[1,128]{1,0:T(1,128)}, s32[1,128]{1,0:T(1,128)}, pred[128]{0:T(512)(128)(4,1)S(1)}, bf16[128,3072]{1,0:T(8,128)(2,1)S(1)}, ...), branch_computations={%region_1.0_spmd, %region_2.3_spmd} | conditional | flops 2457610496 | bytes 95094240 | solution.py:117
  15.7 6.2 %broadcast.198.clone = f32[3072,1024]{1,0:T(8,128)} broadcast(f32[]{:T(128)} %constant.115.clone), dimensions={} | broadcast | bytes 12582916 | tf_op jit(solution)/shard_map/broadcast.9
  24.0 1.8 collective-permute-done.1
  28.3 1.3 collective-permute-start.2
  29.6 9.6 %collective-permute-done.2 = bf16[128,1024]{1,0:T(8,128)(2,1)S(1)} collective-permute-done((bf16[128,1024]{1,0:T(8,128)(2,1)S(1)}, bf16[128,1024]{1,0:T(8,128)(2,1)S(1)}, u32[]{:S(2)}, u32[]{:S(2)}) %collective-permute-start.2) | collective-permute-done | bytes 262176 | tf_op jit(solution)/shard_map/ppermute | solution.py:15
  40.0 7.3 %conditional.5 = (f32[64,1024]{1,0:T(8,128)S(1)}, f32[192,1024]{1,0:T(8,128)}, f32[128,1024]{1,0:T(8,128)S(1)}, f32[3072,1024]{1,0:T(8,128)}) conditional(s32[]{:T(128)} %convert_element_type.158, () %tuple.42, (pred[]{:T(512)}, s32[1,128]{1,0:T(1,128)}, s32[1,128]{1,0:T(1,128)}, pred[128]{0:T(512)(128)(4,1)S(1)}, bf16[128,3072]{1,0:T(8,128)(2,1)S(1)}, ...), branch_computations={%region_4.5_spmd, %region_5.6_spmd} | conditional | flops 2457610496 | bytes 99812880 | solution.py:117
  41.1 6.2 %broadcast.213.clone = f32[3072,1024]{1,0:T(8,128)} broadcast(f32[]{:T(128)} %constant.132.clone), dimensions={} | broadcast | bytes 12582916 | tf_op jit(solution)/shard_map/broadcast.37
  49.5 1.8 collective-permute-done.3
  53.9 1.3 collective-permute-start.4
  55.2 9.9 %collective-permute-done.4 = bf16[128,1024]{1,0:T(8,128)(2,1)S(1)} collective-permute-done((bf16[128,1024]{1,0:T(8,128)(2,1)S(1)}, bf16[128,1024]{1,0:T(8,128)(2,1)S(1)}, u32[]{:S(2)}, u32[]{:S(2)}) %collective-permute-start.4) | collective-permute-done | bytes 262176 | tf_op jit(solution)/shard_map/ppermute | solution.py:15
  65.9 7.2 %conditional.6 = (f32[64,1024]{1,0:T(8,128)S(1)}, f32[192,1024]{1,0:T(8,128)}, f32[128,1024]{1,0:T(8,128)S(1)}, f32[3072,1024]{1,0:T(8,128)}) conditional(s32[]{:T(128)} %convert_element_type.161, () %tuple.44, (pred[]{:T(512)}, s32[1,128]{1,0:T(1,128)}, s32[1,128]{1,0:T(1,128)}, pred[128]{0:T(512)(128)(4,1)S(1)}, bf16[128,3072]{1,0:T(8,128)(2,1)S(1)}, ...), branch_computations={%region_7.8_spmd, %region_8.9_spmd} | conditional | flops 2457610496 | bytes 99812880 | solution.py:117
  67.0 6.1 %broadcast.227.clone = f32[3072,1024]{1,0:T(8,128)} broadcast(f32[]{:T(128)} %constant.175.clone), dimensions={} | broadcast | bytes 12582916 | tf_op jit(solution)/shard_map/broadcast.59
  75.4 1.8 collective-permute-done.5
  81.1 92.4 %collective-permute-done.6 = bf16[128,1024]{1,0:T(8,128)(2,1)S(1)} collective-permute-done((bf16[128,1024]{1,0:T(8,128)(2,1)S(1)}, bf16[128,1024]{1,0:T(8,128)(2,1)S(1)}, u32[]{:S(2)}, u32[]{:S(2)}) %collective-permute-start.6) | collective-permute-done | bytes 262176 | tf_op jit(solution)/shard_map/ppermute | solution.py:15
  174.4 36.3 %conditional.7 = (f32[64,1024]{1,0:T(8,128)S(1)}, f32[192,1024]{1,0:T(8,128)}, f32[128,1024]{1,0:T(8,128)S(1)}, f32[3072,1024]{1,0:T(8,128)}) conditional(s32[]{:T(128)} %convert_element_type.164, () %tuple.46, (pred[]{:T(512)}, s32[1,128]{1,0:T(1,128)}, s32[1,128]{1,0:T(1,128)}, pred[128]{0:T(512)(128)(4,1)S(1)}, ...), branch_computations={%region_10.11_spmd, %region_11.12_spmd} | conditional | flops 2457610496 | bytes 99812880 | solution.py:117
  174.4 3.9 %fusion.187 = f32[128,1024]{1,0:T(8,128)S(1)} fusion(bf16[128,3072]{1,0:T(8,128)(2,1)S(1)} %get-tuple-element.134, bf16[3072,1024]{1,0:T(8,128)(2,1)} %get-tuple-element.135), kind=kOutput, calls=%fused_computation.370 | convolution fusion | flops 805306368 | bytes 7602176 | tf_op jit(solution)/shard_map/cond/branch_1_fun/dot_general | solution.py:73
  178.9 1.5 fusion.138
  181.3 2.2 fusion.188
  184.7 2.8 dynamic_update_slice.34
  188.6 2.9 dynamic_update_slice.35
  191.5 6.4 %convolution_bitcast_fusion.6 = f32[3072,1024]{0,1:T(8,128)} fusion(bf16[128,1024]{1,0:T(8,128)(2,1)S(1)} %get-tuple-element.194, bf16[128,3072]{1,0:T(8,128)(2,1)S(1)} %get-tuple-element.134), kind=kOutput, calls=%fused_computation.243 | convolution fusion | flops 805306368 | bytes 13631488 | tf_op jit(solution)/shard_map/cond/branch_1_fun/dot_general | solution.py:84
  197.9 12.7 %copy.22 = f32[3072,1024]{1,0:T(8,128)} copy(f32[3072,1024]{0,1:T(8,128)} %convolution_bitcast_fusion.6) | data formatting | bytes 25165824 | tf_op jit(solution)/shard_map/cond | solution.py:117
  210.6 1.8 add_convert_fusion.13
  212.5 20.2 %add_convert_fusion.8 = bf16[3072,1024]{1,0:T(8,128)(2,1)} fusion(f32[3072,1024]{1,0:T(8,128)} %get-tuple-element.179, f32[3072,1024]{1,0:T(8,128)} %get-tuple-element.178, f32[3072,1024]{1,0:T(8,128)} %get-tuple-element.176, f32[3072,1024]{1,0:T(8,128)} %get-tuple-element.177), kind=kLoop, calls=%fused_computation.324 | loop fusion | flops 12582912 | bytes 56623104 | tf_op jit(solution)/shard_map/convert_element_type | solution.py:135
  233.5 109.5 %reduce-scatter.5.cloned.1.call-done = bf16[768,1024]{1,0:T(8,128)(2,1)} async-done(((bf16[3072,1024]{1,0:T(8,128)(2,1)}), bf16[768,1024]{1,0:T(8,128)(2,1)}) %reduce-scatter.5.cloned.1.call-update) | async-done | bytes 1572880 | tf_op jit(solution)/shard_map/reduce_scatter | solution.py:134
  345.3 1.9 collective-permute-done.7
  348.6 2.0 fusion.179
  350.6 2.7 reduce-scatter.11.cloned.1.call-done
  353.2 1.3 bitcast_convert_fusion.2
  354.6 11.1 %reduce-scatter.7.cloned.1.call-done = bf16[384,1024]{1,0:T(8,128)(2,1)} async-done(((bf16[768,1024]{1,0:T(8,128)(2,1)}), bf16[384,1024]{1,0:T(8,128)(2,1)}) %reduce-scatter.7.cloned.1.call-update) | async-done | bytes 786448 | tf_op jit(solution)/shard_map/reduce_scatter | solution.py:142
  365.7 2.5 bitcast_convert_fusion
  (99 shorter events, 33.6 us)
Async XLA Ops:
  7.2 225.6 %reduce-scatter.9.cloned.1.call-start = ((), (), s32[]{:S(2)}) async-start(), calls=%async_computation.6 | async-start | bytes 163840 | tf_op jit(solution)/shard_map/reduce_scatter | solution.py:137
  9.4 4.8 %collective-permute-start = (bf16[64,1024]{1,0:T(8,128)(2,1)S(1)}, bf16[64,1024]{1,0:T(8,128)(2,1)S(1)}, u32[]{:S(2)}, u32[]{:S(2)}) collective-permute-start(bf16[64,1024]{1,0:T(8,128)(2,1)S(1)} %slice.112), channel_id=1, source_target_pairs={{0,1},{2,3},{4,5},{6,7},{8,9},{10,11},{12,13},{14,15},{16,17},{18,... | collective-permute-start | bytes 393224 | tf_op jit(solution)/shard_map/ppermute | solution.py:15
  12.8 1.9 copy-start.26
  14.6 11.1 %copy-start.4 = (bf16[1,1,128,1024]{3,2,1,0:T(8,128)(2,1)S(1)}, bf16[1,1,128,1024]{3,2,1,0:T(8,128)(2,1)}, u32[]{:S(2)}) copy-start(bf16[1,1,128,1024]{3,2,1,0:T(8,128)(2,1)} %param.16) | copy-start | bytes 786436
  21.9 18.1 %copy-start.14 = (f32[64,1024]{1,0:T(8,128)}, f32[64,1024]{1,0:T(8,128)S(1)}, u32[]{:S(2)}) copy-start(f32[64,1024]{1,0:T(8,128)S(1)} %get-tuple-element.170) | copy-start | bytes 786436
  22.7 3.1 collective-permute-start.1
  28.3 11.7 %copy-start.20 = (bf16[128,1024]{1,0:T(8,128)(2,1)}, bf16[128,1024]{1,0:T(8,128)(2,1)S(1)}, u32[]{:S(2)}) copy-start(bf16[128,1024]{1,0:T(8,128)(2,1)S(1)} %add_convert_fusion.12) | copy-start | bytes 786436
  28.3 10.9 %collective-permute-start.2 = (bf16[128,1024]{1,0:T(8,128)(2,1)S(1)}, bf16[128,1024]{1,0:T(8,128)(2,1)S(1)}, u32[]{:S(2)}, u32[]{:S(2)}) collective-permute-start(bf16[128,1024]{1,0:T(8,128)(2,1)S(1)} %add_convert_fusion.12), channel_id=1, source_target_pairs={{2,0},{4,2},{6,4},{3,1},{5,3},{7,5},{10,8},{12,10},{14,12},{11,9},... | collective-permute-start | bytes 786440 | tf_op jit(solution)/shard_map/ppermute | solution.py:15
  47.3 18.6 %copy-start.16 = (f32[64,1024]{1,0:T(8,128)}, f32[64,1024]{1,0:T(8,128)S(1)}, u32[]{:S(2)}) copy-start(f32[64,1024]{1,0:T(8,128)S(1)} %get-tuple-element.171) | copy-start | bytes 786436
  48.2 3.1 collective-permute-start.3
  53.9 12.0 %copy-start.22 = (bf16[128,1024]{1,0:T(8,128)(2,1)}, bf16[128,1024]{1,0:T(8,128)(2,1)S(1)}, u32[]{:S(2)}) copy-start(bf16[128,1024]{1,0:T(8,128)(2,1)S(1)} %add_convert_fusion.11) | copy-start | bytes 786436
  53.9 11.2 %collective-permute-start.4 = (bf16[128,1024]{1,0:T(8,128)(2,1)S(1)}, bf16[128,1024]{1,0:T(8,128)(2,1)S(1)}, u32[]{:S(2)}, u32[]{:S(2)}) collective-permute-start(bf16[128,1024]{1,0:T(8,128)(2,1)S(1)} %add_convert_fusion.11), channel_id=1, source_target_pairs={{2,0},{4,2},{6,4},{3,1},{5,3},{7,5},{10,8},{12,10},{14,12},{11,9},... | collective-permute-start | bytes 786440 | tf_op jit(solution)/shard_map/ppermute | solution.py:15
  73.1 101.3 %copy-start.18 = (f32[64,1024]{1,0:T(8,128)}, f32[64,1024]{1,0:T(8,128)S(1)}, u32[]{:S(2)}) copy-start(f32[64,1024]{1,0:T(8,128)S(1)} %get-tuple-element.172) | copy-start | bytes 786436
  74.1 3.1 collective-permute-start.5
  79.8 94.6 %copy-start.24 = (bf16[128,1024]{1,0:T(8,128)(2,1)}, bf16[128,1024]{1,0:T(8,128)(2,1)S(1)}, u32[]{:S(2)}) copy-start(bf16[128,1024]{1,0:T(8,128)(2,1)S(1)} %add_convert_fusion.10) | copy-start | bytes 786436
  79.8 93.7 %collective-permute-start.6 = (bf16[128,1024]{1,0:T(8,128)(2,1)S(1)}, bf16[128,1024]{1,0:T(8,128)(2,1)S(1)}, u32[]{:S(2)}, u32[]{:S(2)}) collective-permute-start(bf16[128,1024]{1,0:T(8,128)(2,1)S(1)} %add_convert_fusion.10), channel_id=1, source_target_pairs={{2,0},{4,2},{6,4},{3,1},{5,3},{7,5},{10,8},{12,10},{14,12},{11,9},... | collective-permute-start | bytes 786440 | tf_op jit(solution)/shard_map/ppermute | solution.py:15
  174.4 3.9 %copy-start.8 = (bf16[64,1024]{1,0:T(8,128)(2,1)S(1)}, bf16[64,1024]{1,0:T(8,128)(2,1)}, u32[]{:S(2)}) copy-start(bf16[64,1024]{1,0:T(8,128)(2,1)} %get-tuple-element.137) | copy-start | bytes 393220 | tf_op jit(solution)/shard_map/cond
  174.4 4.2 %copy-start.29 = (f32[128,1024]{1,0:T(8,128)S(1)}, f32[128,1024]{1,0:T(8,128)}, u32[]{:S(2)}) copy-start(f32[128,1024]{1,0:T(8,128)} %get-tuple-element.133) | copy-start | bytes 1572868 | tf_op jit(solution)/shard_map/cond
  174.4 4.2 %copy-start.44 = (bf16[2,1024]{1,0:T(2,128)(2,1)S(1)}, bf16[2,1024]{1,0:T(2,128)(2,1)}, u32[]{:S(2)}) copy-start(bf16[2,1024]{1,0:T(2,128)(2,1)} %get-tuple-element.138) | copy-start | bytes 12292 | tf_op jit(solution)/shard_map/cond
  174.4 4.5 %copy-start.36 = (s32[1,128]{1,0:T(1,128)S(1)}, s32[1,128]{1,0:T(1,128)}, u32[]{:S(2)}) copy-start(s32[1,128]{1,0:T(1,128)} %get-tuple-element.131) | copy-start | bytes 1540 | tf_op jit(solution)/shard_map/cond
  174.4 4.4 %copy-start.40 = (s32[1,128]{1,0:T(1,128)S(1)}, s32[1,128]{1,0:T(1,128)}, u32[]{:S(2)}) copy-start(s32[1,128]{1,0:T(1,128)} %get-tuple-element.132) | copy-start | bytes 1540 | tf_op jit(solution)/shard_map/cond
  174.4 4.5 %copy-start.30 = (f32[128,1024]{1,0:T(8,128)S(1)}, f32[128,1024]{1,0:T(8,128)}, u32[]{:S(2)}) copy-start(f32[128,1024]{1,0:T(8,128)} %get-tuple-element.139) | copy-start | bytes 1572868 | tf_op jit(solution)/shard_map/cond
  178.3 3.0 copy-start.3
  197.9 12.7 %copy-start.12 = (f32[128,1024]{1,0:T(8,128)S(1)}, f32[128,1024]{1,0:T(8,128)}, u32[]{:S(2)}) copy-start(f32[128,1024]{1,0:T(8,128)} %get-tuple-element.228) | copy-start | bytes 1572868 | tf_op jit(solution)/shard_map/cond
  197.9 12.7 %copy-start.19 = (f32[64,1024]{1,0:T(8,128)S(1)}, f32[64,1024]{1,0:T(8,128)}, u32[]{:S(2)}) copy-start(f32[64,1024]{1,0:T(8,128)} %convolution_bitcast_fusion.7) | copy-start | bytes 786436 | tf_op jit(solution)/shard_map/cond
  212.5 130.6 %reduce-scatter.5.cloned.1.call-start = ((), (), s32[]{:S(2)}) async-start(), calls=%async_computation.4 | async-start | bytes 7864320 | tf_op jit(solution)/shard_map/reduce_scatter | solution.py:134
  232.7 115.8 %copy-start.21 = (bf16[128,1024]{1,0:T(8,128)(2,1)S(1)}, bf16[128,1024]{1,0:T(8,128)(2,1)}, u32[]{:S(2)}) copy-start(bf16[128,1024]{1,0:T(8,128)(2,1)} %copy-done.20) | copy-start | bytes 786436
  232.7 115.8 %copy-start.23 = (bf16[128,1024]{1,0:T(8,128)(2,1)S(1)}, bf16[128,1024]{1,0:T(8,128)(2,1)}, u32[]{:S(2)}) copy-start(bf16[128,1024]{1,0:T(8,128)(2,1)} %copy-done.22) | copy-start | bytes 786436
  232.7 115.8 %copy-start.25 = (bf16[128,1024]{1,0:T(8,128)(2,1)S(1)}, bf16[128,1024]{1,0:T(8,128)(2,1)}, u32[]{:S(2)}) copy-start(bf16[128,1024]{1,0:T(8,128)(2,1)} %copy-done.24) | copy-start | bytes 786436
  232.7 120.5 %reduce-scatter.11.cloned.1.call-start = ((), (), s32[]{:S(2)}) async-start(), calls=%async_computation.7 | async-start | bytes 49152 | tf_op jit(solution)/shard_map/reduce_scatter | solution.py:145
  233.5 132.2 %reduce-scatter.7.cloned.1.call-start = ((), (), s32[]{:S(2)}) async-start(), calls=%async_computation.5 | async-start | bytes 2359296 | tf_op jit(solution)/shard_map/reduce_scatter | solution.py:142
  344.0 3.2 collective-permute-start.7
Sparse Core Ops, SparseCore 0:
  212.6 18.5 reduce-scatter.8
  233.6 109.4 reduce-scatter.4
  345.3 7.9 reduce-scatter.10
  355.4 10.2 reduce-scatter.6
where the time goes:
time: 376 us; the launch traced here: 375 us
  waiting for transfers between devices  243 us (65%)
  other arithmetic  44.9 us (12%)
  local copies, waits for them, and re-layouts  44.8 us (12%)
  matrix products  15.4 us (4%)
  between operations  14.7 us (4%)
  starting transfers between devices  11.5 us (3%)
    ppermute x8, waiting for transfers between devices, from_behind(): return lax.ppermute(array, axis, pairs)  119 us
    reduce_scatter x1, waiting for transfers between devices, on_device(): lax.psum_scatter(conv_total.astype(jnp.bfloat16), 'dp', scatter_dimension...  110 us
    another operation x12, local copies, waits for them, and re-layouts  21.6 us
    convert_element_type x1, other arithmetic, on_device(): conv_total.astype(jnp.bfloat16)  20.2 us
    cond x1, local copies, waits for them, and re-layouts, on_device(): lax.cond(active, active_work, spare_work, incoming)  12.7 us
    ppermute x8, starting transfers between devices, from_behind(): return lax.ppermute(array, axis, pairs)  11.4 us
    reduce_scatter x1, waiting for transfers between devices, on_device(): lax.psum_scatter(conv_mid.astype(jnp.bfloat16), 'seq', scatter_dimension=...  11.1 us
  transfers between devices with their start and end apart: 12, of which 10 were waited for; matrix products, arithmetic and copies ran while one was open for 7% of the time, Pallas kernels for 0%

commit v1 on v0

v1 whole, which is shorter than its diff:
```python
import jax
import jax.numpy as jnp
from jax import lax
from jax.sharding import PartitionSpec as P

KERNEL = 3


EPS = 1e-06


def from_behind(array, axis, by):
    count = lax.axis_size(axis)
    pairs = [(i, i + by) for i in range(count) if 0 <= i + by < count]
    return lax.ppermute(array, axis, pairs)


def head_grad(out_bf, head_weight, click, convert, valid):
    logits = jnp.dot(out_bf, head_weight.T, preferred_element_type=jnp.float32)
    label_y = click.astype(jnp.float32)
    label_z = label_y * convert.astype(jnp.float32)
    weight_m = valid.astype(jnp.float32)

    def event_loss(first, second):
        soft = jax.nn.softplus
        rest = jnp.log(jax.nn.sigmoid(-first) + jax.nn.sigmoid(first) * jax.nn.sigmoid(-second))
        return (
            label_y * soft(-first)
            + (1.0 - label_y) * soft(first)
            + label_z * (soft(-first) + soft(-second))
            - (1.0 - label_z) * rest
        )

    _, pull = jax.vjp(event_loss, logits[:, 0], logits[:, 1])
    grad_first, grad_second = pull(weight_m)
    heads = head_weight.astype(jnp.float32)
    return grad_first[:, None] * heads[0][None] + grad_second[:, None] * heads[1][None]


def on_device(
    section_input, event_ids, lengths, clicks, conversions, conv_weight, type_table, head_weight
):
    inputs_bf = section_input[0, 0]
    rows, width = inputs_bf.shape
    halo_rows = rows // 2
    weight = conv_weight[0]
    table = type_table[0]
    kinds = table.shape[0]
    section = lax.axis_index("pipe")
    sections = lax.axis_size("pipe")
    users, shards = lax.axis_size("dp"), lax.axis_size("seq")
    spacing = jnp.right_shift(jnp.int32(rows // 4), section)
    inputs = inputs_bf.astype(jnp.float32)
    inv_rms = lax.rsqrt(jnp.mean(inputs * inputs, axis=-1, keepdims=True) + EPS)
    normed = inputs * inv_rms
    normed_bf = normed.astype(jnp.bfloat16)
    earlier = from_behind(normed_bf[rows - halo_rows :], "seq", 1)
    normed_all = lax.all_gather(normed_bf, ("dp", "seq"), axis=0, tiled=True)
    ids_all = lax.all_gather(event_ids[0], ("dp", "seq"), axis=0, tiled=True)
    extended = jnp.concatenate([earlier, normed_bf], axis=0)
    onehot = (event_ids[0][:, None] == jnp.arange(kinds, dtype=jnp.int32)[None, :]).astype(
        jnp.bfloat16
    )
    position = lax.axis_index("seq") * rows + jnp.arange(rows, dtype=jnp.int32)
    valid = position < lengths[0]
    is_last = section == sections - 1

    pre = jnp.dot(onehot, table, preferred_element_type=jnp.float32)
    for tap in range(KERNEL):
        shifted = lax.dynamic_slice_in_dim(extended, halo_rows - tap * spacing, rows, 0)
        pre = pre + jnp.dot(
            shifted, weight[tap * width : (tap + 1) * width], preferred_element_type=jnp.float32
        )
    active, pull = jax.vjp(jax.nn.gelu, pre)
    slope = pull(jnp.ones_like(pre))[0]
    out_bf = (inputs + active).astype(jnp.bfloat16)
    top_grad = head_grad(out_bf, head_weight, clicks[0], conversions[0], valid)

    incoming = jnp.zeros((rows, width), jnp.bfloat16)
    for tick in range(sections):
        grad_out = jnp.where(is_last, top_grad, incoming.astype(jnp.float32))
        grad_pre = (grad_out * slope).astype(jnp.bfloat16)
        later = from_behind(grad_pre[:halo_rows], "seq", -1)
        grad_ext = jnp.concatenate([grad_pre, later], axis=0)
        grad_normed = jnp.zeros((rows, width), jnp.float32)
        for tap in range(KERNEL):
            shifted = lax.dynamic_slice_in_dim(grad_ext, tap * spacing, rows, 0)
            grad_normed = grad_normed + lax.dot_general(
                shifted,
                weight[tap * width : (tap + 1) * width],
                (((1,), (1,)), ((), ())),
                preferred_element_type=jnp.float32,
            )
        inner = jnp.mean(grad_normed * normed, axis=-1, keepdims=True)
        grad_in = (grad_out + inv_rms * (grad_normed - normed * inner)).astype(jnp.bfloat16)
        if tick + 1 < sections:
            incoming = from_behind(grad_in, "pipe", -1)

    grad_all = lax.all_gather(grad_pre, ("dp", "seq"), axis=0, tiled=True)
    owner = lax.axis_index("dp") * shards + lax.axis_index("seq")
    share = KERNEL * width // (users * shards)
    start = owner * share
    wide = jnp.concatenate([normed_all, normed_all], axis=1)
    mine = lax.dynamic_slice_in_dim(wide, lax.rem(start, width), share, 1)
    mine = mine.reshape(users, shards * rows, share)
    tap_of = lax.div(start + jnp.arange(share, dtype=jnp.int32), width)
    padded = jnp.pad(mine, ((0, 0), (2 * halo_rows, 0), (0, 0)))
    part = mine
    for tap in range(1, KERNEL):
        moved = lax.dynamic_slice_in_dim(
            padded, 2 * halo_rows - tap * spacing, shards * rows, 1
        )
        part = jnp.where((tap_of == tap)[None, None, :], moved, part)
    part = part.reshape(users * shards * rows, share)
    conv_share = lax.dot_general(
        part, grad_all, (((0,), (0,)), ((), ())), preferred_element_type=jnp.float32
    )
    kind_share = kinds // (users * shards)
    kind = owner * kind_share + jnp.arange(kind_share, dtype=jnp.int32)
    picks = (ids_all[:, None] == kind[None, :]).astype(jnp.bfloat16)
    type_share = lax.dot_general(
        picks, grad_all, (((0,), (0,)), ((), ())), preferred_element_type=jnp.float32
    )
    return (conv_share[None], type_share[None], grad_in[None, None])


def solution(mesh):
    placed = (
        P("pipe", "dp", "seq", None),
        P("dp", "seq"),
        P("dp"),
        P("dp", "seq"),
        P("dp", "seq"),
        P("pipe", None, None),
        P("pipe", None, None),
        P(),
    )
    return jax.shard_map(
        on_device,
        mesh=mesh,
        in_specs=placed,
        out_specs=(
            P("pipe", ("dp", "seq"), None),
            P("pipe", ("dp", "seq"), None),
            P("pipe", "dp", "seq", None),
        ),
        check_vma=False,
    )
```

time: 376 us -> 122 us (0.32)
  waiting for transfers between devices: 243 us -> 39.7 us
  local copies, waits for them, and re-layouts: 44.8 us -> 1.08 us
  other arithmetic: 44.9 us -> 8.61 us
  matrix products: 15.4 us -> 32.8 us
  blocking collectives: 0 us -> 12.2 us
    reduce_scatter x4 -> x0, waiting for transfers between devices: 123 us -> none  [the longest x1 110 us: on_device(): lax.psum_scatter(conv_total.astype(jnp.bfloat16), 'dp', scatter_dimension...]
    ppermute x8, waiting for transfers between devices: 119 us -> 34.2 us  [from_behind(): return lax.ppermute(array, axis, pairs)]
    convert_element_type x7 -> x4, other arithmetic: 26.4 us -> 2.44 us  [on_device(): grad_pre = (grad_out * slope).astype(jnp.bfloat16)]
    another operation x12 -> x0, local copies, waits for them, and re-layouts: 21.6 us -> none
    dot_general x6 -> x18, matrix products: 15.1 us -> 32.4 us  [the longest x12 20.5 us: on_device(): lax.dot_general(shifted, weight[tap * width:(tap + 1) * width], (((1,), (...]
    cond x19 -> x0, local copies, waits for them, and re-layouts: 12.8 us -> none  [the longest x1 12.7 us: on_device(): lax.cond(active, active_work, spare_work, incoming)]
    all_gather x0 -> x1, blocking collectives: none -> 12.2 us  [on_device(): ids_all = lax.all_gather(event_ids[0], ('dp', 'seq'), axis=0, tiled=True)]
    dynamic_update_slice x3 -> x0, local copies, waits for them, and re-layouts: 6.68 us -> none  [active_work(): lax.dynamic_update_slice_in_dim(grad_ext, current + grad_taps[:, tap * wi...]
  transfers between devices with their start and end apart: 12 -> 10, of which waited for: 10 -> 7; matrix products, arithmetic and copies ran while one was open for 7% -> 23% of each run, Pallas kernels for 0% -> 0%
where the time goes in v1:
time: 122 us; the launch traced here: 121 us
  waiting for transfers between devices  39.7 us (33%)
  matrix products  32.8 us (27%)
  between operations  15.2 us (12%)
  blocking collectives  12.2 us (10%)
  starting transfers between devices  11.5 us (9%)
  other arithmetic  8.61 us (7%)
    ppermute x8, waiting for transfers between devices, from_behind(): return lax.ppermute(array, axis, pairs)  34.2 us
    dot_general x12, matrix products, on_device(): lax.dot_general(shifted, weight[tap * width:(tap + 1) * width], (((1,), (...  20.5 us
    all_gather x1, blocking collectives, on_device(): ids_all = lax.all_gather(event_ids[0], ('dp', 'seq'), axis=0, tiled=True)  12.2 us
    ppermute x8, starting transfers between devices, from_behind(): return lax.ppermute(array, axis, pairs)  11.4 us
    dot_general x3, matrix products, on_device(): jnp.dot(shifted, weight[tap * width:(tap + 1) * width], preferred_element...  6.59 us
    all_gather x1, waiting for transfers between devices, on_device(): grad_all = lax.all_gather(grad_pre, ('dp', 'seq'), axis=0, tiled=True)  5.47 us
    dot_general x1, matrix products, on_device(): lax.dot_general(part, grad_all, (((0,), (0,)), ((), ())), preferred_eleme...  3.88 us
  transfers between devices with their start and end apart: 10, of which 7 were waited for; matrix products, arithmetic and copies ran while one was open for 23% of the time, Pallas kernels for 0%

profile of v1, /device:TPU:0, one launch (start us, length us, event | category | flops | bytes accessed | tf_op | source)
XLA Modules:
  0.0 121.1 jit_solution(3764307851698369551)
XLA Ops:
  7.2 1.1 fusion.110
  8.3 1.1 fusion.89
  9.4 2.4 %collective-permute-start = (bf16[64,1024]{1,0:T(8,128)(2,1)S(1)}, bf16[64,1024]{1,0:T(8,128)(2,1)S(1)}, u32[]{:S(2)}, u32[]{:S(2)}) collective-permute-start(bf16[64,1024]{1,0:T(8,128)(2,1)S(1)} %slice.72), channel_id=1, source_target_pairs={{0,1},{2,3},{4,5},{6,7},{8,9},{10,11},{12,13},{14,15},{16,17},{18,... | collective-permute-start | bytes 393224 | tf_op jit(solution)/shard_map/ppermute | solution.py:15
  11.8 2.2 %fusion.28 = f32[128,1024]{1,0:T(8,128)S(1)} fusion(bf16[1,3072,1024]{2,1,0:T(8,128)(2,1)} %param.13, bf16[1,1,128,1024]{3,2,1,0:T(8,128)(2,1)} %param.8, f32[128]{0:T(128)S(1)} %add_rsqrt_fusion), kind=kOutput, calls=%fused_computation.30 | convolution fusion | flops 268828672 | bytes 2884096 | tf_op jit(solution)/shard_map/dot_general | solution.py:71
  15.1 2.1 %fusion.8 = f32[128,1024]{1,0:T(8,128)S(1)} fusion(bf16[1,3072,1024]{2,1,0:T(8,128)(2,1)} %param.13, s32[]{:T(128)S(6)} %select_n.103, bf16[128,1024]{1,0:T(8,128)(2,1)S(1)} %fusion.89, bf16[64,1024]{1,0:T(8,128)(2,1)S(1)} %collective-permute-done), kind=kOutput, calls=%fused_computation.10 | convolution fusion | flops 268959744 | bytes 3014660 | tf_op jit(solution)/shard_map/dot_general | solution.py:71
  17.2 2.3 %fusion.51 = f32[128,1024]{1,0:T(8,128)S(1)} fusion(f32[128,1024]{1,0:T(8,128)S(1)} %fusion.8, f32[128,1024]{1,0:T(8,128)S(1)} %convolution_add_fusion, bf16[1,3072,1024]{2,1,0:T(8,128)(2,1)} %param.13, s32[]{:T(128)S(6)} %select_n.102, bf16[128,1024]{1,0:T(8,128)(2,1)S(1)} %fusion.89, bf16[64,1024]{1,0:T(8,128)(2,1)S(1)} %collective-permute-done), kind=kOutput, calls=%fused_computation.41 | convolution fusion | flops 269221888 | bytes 4063236 | tf_op jit(solution)/shard_map/dot_general | solution.py:71
  20.3 1.3 %collective-permute-start.1 = (bf16[64,1024]{1,0:T(8,128)(2,1)S(1)}, bf16[64,1024]{1,0:T(8,128)(2,1)S(1)}, u32[]{:S(2)}, u32[]{:S(2)}) collective-permute-start(bf16[64,1024]{1,0:T(8,128)(2,1)S(1)} %slice.75), channel_id=1, source_target_pairs={{1,0},{3,2},{5,4},{7,6},{9,8},{11,10},{13,12},{15,14},{17,16},{19,... | collective-permute-start | bytes 393224 | tf_op jit(solution)/shard_map/ppermute | solution.py:15
  22.5 1.1 collective-permute-done.1
  24.4 1.0 fusion.90
  25.7 1.3 %collective-permute-start.2 = (bf16[128,1024]{1,0:T(8,128)(2,1)S(1)}, bf16[128,1024]{1,0:T(8,128)(2,1)S(1)}, u32[]{:S(2)}, u32[]{:S(2)}) collective-permute-start(bf16[128,1024]{1,0:T(8,128)(2,1)S(1)} %fusion.94), channel_id=1, source_target_pairs={{2,0},{4,2},{6,4},{3,1},{5,3},{7,5},{10,8},{12,10},{14,12},{11,9},... | collective-permute-start | bytes 786440 | tf_op jit(solution)/shard_map/ppermute | solution.py:15
  27.0 9.5 %collective-permute-done.2 = bf16[128,1024]{1,0:T(8,128)(2,1)S(1)} collective-permute-done((bf16[128,1024]{1,0:T(8,128)(2,1)S(1)}, bf16[128,1024]{1,0:T(8,128)(2,1)S(1)}, u32[]{:S(2)}, u32[]{:S(2)}) %collective-permute-start.2) | collective-permute-done | bytes 262176 | tf_op jit(solution)/shard_map/ppermute | solution.py:15
  37.0 1.3 %collective-permute-start.3 = (bf16[64,1024]{1,0:T(8,128)(2,1)S(1)}, bf16[64,1024]{1,0:T(8,128)(2,1)S(1)}, u32[]{:S(2)}, u32[]{:S(2)}) collective-permute-start(bf16[64,1024]{1,0:T(8,128)(2,1)S(1)} %slice.76), channel_id=1, source_target_pairs={{1,0},{3,2},{5,4},{7,6},{9,8},{11,10},{13,12},{15,14},{17,16},{19,... | collective-permute-start | bytes 393224 | tf_op jit(solution)/shard_map/ppermute | solution.py:15
  38.4 1.9 %collective-permute-done.3 = bf16[64,1024]{1,0:T(8,128)(2,1)S(1)} collective-permute-done((bf16[64,1024]{1,0:T(8,128)(2,1)S(1)}, bf16[64,1024]{1,0:T(8,128)(2,1)S(1)}, u32[]{:S(2)}, u32[]{:S(2)}) %collective-permute-start.3) | collective-permute-done | bytes 131104 | tf_op jit(solution)/shard_map/ppermute | solution.py:15
  40.2 2.6 %fusion.4 = f32[128,1024]{1,0:T(8,128)S(1)} fusion(bf16[1,3072,1024]{2,1,0:T(8,128)(2,1)} %param.13, s32[]{:T(128)S(6)} %select_n.115, bf16[128,1024]{1,0:T(8,128)(2,1)S(1)} %multiply_convert_fusion.2, bf16[64,1024]{1,0:T(8,128)(2,1)S(1)} %collective-permute-done.3), kind=kOutput, calls=%fused_computation.6 | convolution fusion | flops 268959744 | bytes 3014660 | tf_op jit(solution)/shard_map/dot_general | solution.py:88
  42.8 2.6 %fusion.14 = f32[128,1024]{1,0:T(8,128)S(1)} fusion(bf16[1,3072,1024]{2,1,0:T(8,128)(2,1)} %param.13, s32[]{:T(128)S(6)} %select_n.114, bf16[128,1024]{1,0:T(8,128)(2,1)S(1)} %multiply_convert_fusion.2, bf16[64,1024]{1,0:T(8,128)(2,1)S(1)} %collective-permute-done.3), kind=kOutput, calls=%fused_computation.16 | convolution fusion | flops 268959744 | bytes 3014660 | tf_op jit(solution)/shard_map/dot_general | solution.py:88
  45.4 2.5 %fusion.95 = (f32[128]{0:T(128)S(1)}, f32[128,1024]{1,0:T(8,128)S(1)}) fusion(bf16[1,1,128,1024]{3,2,1,0:T(8,128)(2,1)S(1)} %copy-done.1, f32[128]{0:T(128)S(1)} %add_rsqrt_fusion, f32[128,1024]{1,0:T(8,128)S(1)} %fusion.4, f32[128,1024]{1,0:T(8,128)S(1)} %fusion.14, bf16[128,1024]{1,0:T(8,128)(2,1)S(1)} %multiply_convert_fusion.2, ...), kind=kOutput, calls=%fused_computation.86 | convolution fusion | flops 269221760 | bytes 4195328 | tf_op jit(solution)/shard_map/dot_general | solution.py:88
  48.2 1.3 %collective-permute-start.4 = (bf16[128,1024]{1,0:T(8,128)(2,1)S(1)}, bf16[128,1024]{1,0:T(8,128)(2,1)S(1)}, u32[]{:S(2)}, u32[]{:S(2)}) collective-permute-start(bf16[128,1024]{1,0:T(8,128)(2,1)S(1)} %fusion.99), channel_id=1, source_target_pairs={{2,0},{4,2},{6,4},{3,1},{5,3},{7,5},{10,8},{12,10},{14,12},{11,9},... | collective-permute-start | bytes 786440 | tf_op jit(solution)/shard_map/ppermute | solution.py:15
  49.5 9.9 %collective-permute-done.4 = bf16[128,1024]{1,0:T(8,128)(2,1)S(1)} collective-permute-done((bf16[128,1024]{1,0:T(8,128)(2,1)S(1)}, bf16[128,1024]{1,0:T(8,128)(2,1)S(1)}, u32[]{:S(2)}, u32[]{:S(2)}) %collective-permute-start.4) | collective-permute-done | bytes 262176 | tf_op jit(solution)/shard_map/ppermute | solution.py:15
  59.9 1.3 %collective-permute-start.5 = (bf16[64,1024]{1,0:T(8,128)(2,1)S(1)}, bf16[64,1024]{1,0:T(8,128)(2,1)S(1)}, u32[]{:S(2)}, u32[]{:S(2)}) collective-permute-start(bf16[64,1024]{1,0:T(8,128)(2,1)S(1)} %slice.77), channel_id=1, source_target_pairs={{1,0},{3,2},{5,4},{7,6},{9,8},{11,10},{13,12},{15,14},{17,16},{19,... | collective-permute-start | bytes 393224 | tf_op jit(solution)/shard_map/ppermute | solution.py:15
  61.2 1.9 %collective-permute-done.5 = bf16[64,1024]{1,0:T(8,128)(2,1)S(1)} collective-permute-done((bf16[64,1024]{1,0:T(8,128)(2,1)S(1)}, bf16[64,1024]{1,0:T(8,128)(2,1)S(1)}, u32[]{:S(2)}, u32[]{:S(2)}) %collective-permute-start.5) | collective-permute-done | bytes 131104 | tf_op jit(solution)/shard_map/ppermute | solution.py:15
  66.1 1.3 %collective-permute-start.6 = (bf16[128,1024]{1,0:T(8,128)(2,1)S(1)}, bf16[128,1024]{1,0:T(8,128)(2,1)S(1)}, u32[]{:S(2)}, u32[]{:S(2)}) collective-permute-start(bf16[128,1024]{1,0:T(8,128)(2,1)S(1)} %fusion.104), channel_id=1, source_target_pairs={{2,0},{4,2},{6,4},{3,1},{5,3},{7,5},{10,8},{12,10},{14,12},{11,9},... | collective-permute-start | bytes 786440 | tf_op jit(solution)/shard_map/ppermute | solution.py:15
  67.4 9.8 %collective-permute-done.6 = bf16[128,1024]{1,0:T(8,128)(2,1)S(1)} collective-permute-done((bf16[128,1024]{1,0:T(8,128)(2,1)S(1)}, bf16[128,1024]{1,0:T(8,128)(2,1)S(1)}, u32[]{:S(2)}, u32[]{:S(2)}) %collective-permute-start.6) | collective-permute-done | bytes 262176 | tf_op jit(solution)/shard_map/ppermute | solution.py:15
  77.2 1.2 multiply_convert_fusion
  79.4 1.3 %collective-permute-start.7 = (bf16[64,1024]{1,0:T(8,128)(2,1)S(1)}, bf16[64,1024]{1,0:T(8,128)(2,1)S(1)}, u32[]{:S(2)}, u32[]{:S(2)}) collective-permute-start(bf16[64,1024]{1,0:T(8,128)(2,1)S(1)} %slice.78), channel_id=1, source_target_pairs={{1,0},{3,2},{5,4},{7,6},{9,8},{11,10},{13,12},{15,14},{17,16},{19,... | collective-permute-start | bytes 393224 | tf_op jit(solution)/shard_map/ppermute | solution.py:15
  80.7 12.2 %all-gather = s32[1,1024]{1,0:T(1,128)S(1)} all-gather(s32[1,128]{1,0:T(1,128)S(1)} %copy-done.7), channel_id=2, replica_groups=mesh['dp'=4,'pipe'=4,'seq'=2] {'dp','seq'}, dimensions={1}, use_global_device_ids=true | all-gather | bytes 4608 | tf_op jit(solution)/shard_map/all_gather | solution.py:59
  93.0 2.6 %fusion = f32[128,1024]{1,0:T(8,128)S(1)} fusion(bf16[1,3072,1024]{2,1,0:T(8,128)(2,1)} %param.13, s32[]{:T(128)S(6)} %select_n.115, bf16[128,1024]{1,0:T(8,128)(2,1)} %multiply_convert_fusion, bf16[64,1024]{1,0:T(8,128)(2,1)S(1)} %collective-permute-done.7), kind=kOutput, calls=%fused_computation.2 | convolution fusion | flops 268959744 | bytes 3014660 | tf_op jit(solution)/shard_map/dot_general | solution.py:88
  95.5 2.4 %fusion.10 = f32[128,1024]{1,0:T(8,128)S(1)} fusion(bf16[1,3072,1024]{2,1,0:T(8,128)(2,1)} %param.13, s32[]{:T(128)S(6)} %select_n.114, bf16[128,1024]{1,0:T(8,128)(2,1)S(1)} %copy-done.4, bf16[64,1024]{1,0:T(8,128)(2,1)S(1)} %collective-permute-done.7), kind=kOutput, calls=%fused_computation.12 | convolution fusion | flops 268959744 | bytes 3014660 | tf_op jit(solution)/shard_map/dot_general | solution.py:88
  98.0 2.5 %fusion.105 = (f32[128]{0:T(128)S(1)}, f32[128,1024]{1,0:T(8,128)S(1)}) fusion(bf16[1,1,128,1024]{3,2,1,0:T(8,128)(2,1)S(1)} %copy-done.1, f32[128]{0:T(128)S(1)} %add_rsqrt_fusion, f32[128,1024]{1,0:T(8,128)S(1)} %fusion, f32[128,1024]{1,0:T(8,128)S(1)} %fusion.10, bf16[128,1024]{1,0:T(8,128)(2,1)S(1)} %copy-done.4, bf16[1,3072,1024]{2,1,0:T(8,128)(2,1)} %param.13), kind=kOutput, calls=%fused_computation.96 | convolution fusion | flops 269221760 | bytes 4195328 | tf_op jit(solution)/shard_map/dot_general | solution.py:88
  101.5 1.5 %fusion.77 = bf16[1024,384]{1,0:T(8,128)(2,1)S(1)} fusion(s32[]{:T(128)S(6)} %select_n.96, bf16[1024,1024]{1,0:T(8,128)(2,1)} %all-gather.4.cloned.1.call-done), kind=kLoop, calls=%fused_computation.64 | loop fusion | flops 1572864 | bytes 2883588 | tf_op jit(solution)/shard_map/concatenate | solution.py:103
  103.7 5.5 %all-gather.6.cloned.1.call-done = bf16[1024,1024]{1,0:T(8,128)(2,1)} async-done(((bf16[128,1024]{1,0:T(8,128)(2,1)}), bf16[1024,1024]{1,0:T(8,128)(2,1)}) %all-gather.6.cloned.1.call-update) | async-done | bytes 2097168 | tf_op jit(solution)/shard_map/all_gather | solution.py:99
  109.2 3.9 %convolution_bitcast_fusion = f32[1,384,1024]{2,1,0:T(8,128)} fusion(bf16[1024,384]{1,0:T(8,128)(2,1)S(1)} %bitcast.213, bf16[1024,1024]{1,0:T(8,128)(2,1)} %all-gather.6.cloned.1.call-done), kind=kOutput, calls=%fused_computation.32 | convolution fusion | flops 805306368 | bytes 4456448 | tf_op jit(solution)/shard_map/dot_general | solution.py:115
  113.0 1.2 convolution_bitcast_fusion.1
  (61 shorter events, 9.9 us)
Async XLA Ops:
  7.2 7.6 %copy-start = (bf16[1,64,1024]{2,1,0:T(8,128)(2,1)S(1)}, bf16[1,64,1024]{2,1,0:T(8,128)(2,1)}, u32[]{:S(2)}) copy-start(bf16[1,64,1024]{2,1,0:T(8,128)(2,1)} %param.14) | copy-start | bytes 393220
  7.2 7.5 %copy-start.7 = (s32[1,128]{1,0:T(1,128)S(1)}, s32[1,128]{1,0:T(1,128)}, u32[]{:S(2)}) copy-start(s32[1,128]{1,0:T(1,128)} %param.9) | copy-start | bytes 1540
  7.2 94.3 %all-gather.4.cloned.1.call-start = ((), (), s32[]{:S(2)}) async-start(), calls=%async_computation | async-start | bytes 2359296 | tf_op jit(solution)/shard_map/all_gather | solution.py:58
  9.4 7.8 %copy-start.5 = (bf16[128,1024]{1,0:T(8,128)(2,1)}, bf16[128,1024]{1,0:T(8,128)(2,1)S(1)}, u32[]{:S(2)}) copy-start(bf16[128,1024]{1,0:T(8,128)(2,1)S(1)} %fusion.89) | copy-start | bytes 786436
  9.4 5.6 %collective-permute-start = (bf16[64,1024]{1,0:T(8,128)(2,1)S(1)}, bf16[64,1024]{1,0:T(8,128)(2,1)S(1)}, u32[]{:S(2)}, u32[]{:S(2)}) collective-permute-start(bf16[64,1024]{1,0:T(8,128)(2,1)S(1)} %slice.72), channel_id=1, source_target_pairs={{0,1},{2,3},{4,5},{6,7},{8,9},{10,11},{12,13},{14,15},{16,17},{18,... | collective-permute-start | bytes 393224 | tf_op jit(solution)/shard_map/ppermute | solution.py:15
  11.8 3.2 %copy-start.6 = (bf16[2,1024]{1,0:T(2,128)(2,1)S(1)}, bf16[2,1024]{1,0:T(2,128)(2,1)}, u32[]{:S(2)}) copy-start(bf16[2,1024]{1,0:T(2,128)(2,1)} %param.15) | copy-start | bytes 12292
  15.1 4.8 %copy-start.8 = (s32[1,128]{1,0:T(1,128)S(1)}, s32[1,128]{1,0:T(1,128)}, u32[]{:S(2)}) copy-start(s32[1,128]{1,0:T(1,128)} %param.11) | copy-start | bytes 1540
  15.1 4.8 %copy-start.9 = (s32[1,128]{1,0:T(1,128)S(1)}, s32[1,128]{1,0:T(1,128)}, u32[]{:S(2)}) copy-start(s32[1,128]{1,0:T(1,128)} %param.12) | copy-start | bytes 1540
  17.2 2.3 %copy-start.1 = (bf16[1,1,128,1024]{3,2,1,0:T(8,128)(2,1)S(1)}, bf16[1,1,128,1024]{3,2,1,0:T(8,128)(2,1)}, u32[]{:S(2)}) copy-start(bf16[1,1,128,1024]{3,2,1,0:T(8,128)(2,1)} %param.8) | copy-start | bytes 786436
  17.2 4.4 %copy-start.2 = (bf16[1,3072,1024]{2,1,0:T(8,128)(2,1)S(1)}, bf16[1,3072,1024]{2,1,0:T(8,128)(2,1)}, u32[]{:S(2)}) copy-start(bf16[1,3072,1024]{2,1,0:T(8,128)(2,1)} %param.13) | copy-start | bytes 18874372
  20.3 3.2 %collective-permute-start.1 = (bf16[64,1024]{1,0:T(8,128)(2,1)S(1)}, bf16[64,1024]{1,0:T(8,128)(2,1)S(1)}, u32[]{:S(2)}, u32[]{:S(2)}) collective-permute-start(bf16[64,1024]{1,0:T(8,128)(2,1)S(1)} %slice.75), channel_id=1, source_target_pairs={{1,0},{3,2},{5,4},{7,6},{9,8},{11,10},{13,12},{15,14},{17,16},{19,... | collective-permute-start | bytes 393224 | tf_op jit(solution)/shard_map/ppermute | solution.py:15
  25.7 10.8 %collective-permute-start.2 = (bf16[128,1024]{1,0:T(8,128)(2,1)S(1)}, bf16[128,1024]{1,0:T(8,128)(2,1)S(1)}, u32[]{:S(2)}, u32[]{:S(2)}) collective-permute-start(bf16[128,1024]{1,0:T(8,128)(2,1)S(1)} %fusion.94), channel_id=1, source_target_pairs={{2,0},{4,2},{6,4},{3,1},{5,3},{7,5},{10,8},{12,10},{14,12},{11,9},... | collective-permute-start | bytes 786440 | tf_op jit(solution)/shard_map/ppermute | solution.py:15
  37.0 3.2 %collective-permute-start.3 = (bf16[64,1024]{1,0:T(8,128)(2,1)S(1)}, bf16[64,1024]{1,0:T(8,128)(2,1)S(1)}, u32[]{:S(2)}, u32[]{:S(2)}) collective-permute-start(bf16[64,1024]{1,0:T(8,128)(2,1)S(1)} %slice.76), channel_id=1, source_target_pairs={{1,0},{3,2},{5,4},{7,6},{9,8},{11,10},{13,12},{15,14},{17,16},{19,... | collective-permute-start | bytes 393224 | tf_op jit(solution)/shard_map/ppermute | solution.py:15
  38.3 70.8 %all-gather.6.cloned.1.call-start = ((), (), s32[]{:S(2)}) async-start(), calls=%async_computation.1 | async-start | bytes 2359296 | tf_op jit(solution)/shard_map/all_gather | solution.py:99
  40.2 22.9 %slice-start = ((s8[6291456]{0:T(1024)(128)(4,1)}), s8[4194304]{0:T(1024)(128)(4,1)S(1)}, s32[]{:S(2)}) async-start(s8[6291456]{0:T(1024)(128)(4,1)} %bitcast.210), calls=%async_computation.2 | async-start | bytes 8388608
  42.8 20.4 %slice-start.1 = ((s8[6291456]{0:T(1024)(128)(4,1)}), s8[2097152]{0:T(1024)(128)(4,1)S(1)}, s32[]{:S(2)}) async-start(s8[6291456]{0:T(1024)(128)(4,1)} %bitcast.210), calls=%async_computation.3 | async-start | bytes 4194304
  48.2 11.2 %collective-permute-start.4 = (bf16[128,1024]{1,0:T(8,128)(2,1)S(1)}, bf16[128,1024]{1,0:T(8,128)(2,1)S(1)}, u32[]{:S(2)}, u32[]{:S(2)}) collective-permute-start(bf16[128,1024]{1,0:T(8,128)(2,1)S(1)} %fusion.99), channel_id=1, source_target_pairs={{2,0},{4,2},{6,4},{3,1},{5,3},{7,5},{10,8},{12,10},{14,12},{11,9},... | collective-permute-start | bytes 786440 | tf_op jit(solution)/shard_map/ppermute | solution.py:15
  59.9 3.2 %collective-permute-start.5 = (bf16[64,1024]{1,0:T(8,128)(2,1)S(1)}, bf16[64,1024]{1,0:T(8,128)(2,1)S(1)}, u32[]{:S(2)}, u32[]{:S(2)}) collective-permute-start(bf16[64,1024]{1,0:T(8,128)(2,1)S(1)} %slice.77), channel_id=1, source_target_pairs={{1,0},{3,2},{5,4},{7,6},{9,8},{11,10},{13,12},{15,14},{17,16},{19,... | collective-permute-start | bytes 393224 | tf_op jit(solution)/shard_map/ppermute | solution.py:15
  66.1 11.1 %collective-permute-start.6 = (bf16[128,1024]{1,0:T(8,128)(2,1)S(1)}, bf16[128,1024]{1,0:T(8,128)(2,1)S(1)}, u32[]{:S(2)}, u32[]{:S(2)}) collective-permute-start(bf16[128,1024]{1,0:T(8,128)(2,1)S(1)} %fusion.104), channel_id=1, source_target_pairs={{2,0},{4,2},{6,4},{3,1},{5,3},{7,5},{10,8},{12,10},{14,12},{11,9},... | collective-permute-start | bytes 786440 | tf_op jit(solution)/shard_map/ppermute | solution.py:15
  78.4 17.1 %copy-start.4 = (bf16[128,1024]{1,0:T(8,128)(2,1)S(1)}, bf16[128,1024]{1,0:T(8,128)(2,1)}, u32[]{:S(2)}) copy-start(bf16[128,1024]{1,0:T(8,128)(2,1)} %multiply_convert_fusion) | copy-start | bytes 786436
  79.4 13.6 %collective-permute-start.7 = (bf16[64,1024]{1,0:T(8,128)(2,1)S(1)}, bf16[64,1024]{1,0:T(8,128)(2,1)S(1)}, u32[]{:S(2)}, u32[]{:S(2)}) collective-permute-start(bf16[64,1024]{1,0:T(8,128)(2,1)S(1)} %slice.78), channel_id=1, source_target_pairs={{1,0},{3,2},{5,4},{7,6},{9,8},{11,10},{13,12},{15,14},{17,16},{19,... | collective-permute-start | bytes 393224 | tf_op jit(solution)/shard_map/ppermute | solution.py:15
  109.1 3.9 %copy-start.3 = (bf16[1024,1024]{1,0:T(8,128)(2,1)S(1)}, bf16[1024,1024]{1,0:T(8,128)(2,1)}, u32[]{:S(2)}) copy-start(bf16[1024,1024]{1,0:T(8,128)(2,1)} %all-gather.6.cloned.1.call-done) | copy-start | bytes 6291460
Sparse Core Ops, SparseCore 0:
  38.4 31.2 all-gather.3
  78.5 30.5 all-gather.5

commit v2 on v1

v2 whole, which is shorter than its diff:
```python
import functools

import jax
import jax.numpy as jnp
from jax import lax
from jax.experimental import pallas as pl
from jax.experimental.pallas import tpu as pltpu
from jax.sharding import PartitionSpec as P

KERNEL = 3
EPS = 1e-06
BLOCK = 256
MESH = pl.DeviceIdType.MESH


def kernel(
    users, shards, sections, kind_share,
    x_ref, row_ref, weight_hbm, table_ref, head_ref,
    conv_ref, type_ref, gin_ref,
    weight_ref, ext, taps, back, tap_src, tap_all, slope, gnorm, gout, gp_all, halo_out, halo_in,
    back_in, inc, gin_buf,
    w_sem, halo_sem, back_sem, pipe_sem, tap_send, tap_recv, dp_send, dp_recv, f_send, f_recv,
):
    rows, width = x_ref.shape
    half = rows // 2
    dp, section, seq = lax.axis_index("dp"), lax.axis_index("pipe"), lax.axis_index("seq")
    group = users * shards
    me = dp * shards + seq
    share = KERNEL * width // group
    is_last = section == sections - 1
    f32, bf16 = jnp.float32, jnp.bfloat16

    for tap in range(KERNEL):
        part = pl.ds(tap * width, width)
        pltpu.make_async_copy(weight_hbm.at[part], weight_ref.at[part], w_sem.at[tap]).start()

    barrier = pltpu.get_barrier_semaphore()

    def peer_id(i):
        peer = lax.rem(me + i, group)
        return peer, lax.div(peer, shards), lax.rem(peer, shards)

    @pl.loop(1, group)
    def _(i):
        _, d, s = peer_id(i)
        pl.semaphore_signal(barrier, inc=1, device_id={"dp": d, "seq": s}, device_id_type=MESH)

    @pl.when(section > 0)
    def _():
        pl.semaphore_signal(barrier, inc=1, device_id={"pipe": section - 1}, device_id_type=MESH)

    @pl.when(section < sections - 1)
    def _():
        pl.semaphore_signal(barrier, inc=1, device_id={"pipe": section + 1}, device_id_type=MESH)

    x = x_ref[...].astype(f32)
    inv = lax.rsqrt(jnp.mean(x * x, axis=-1, keepdims=True) + EPS)
    normed = x * inv
    normed_bf = normed.astype(bf16)
    halo_out[...] = normed_bf[half:]

    pipe_peers = (section > 0).astype(jnp.int32) + (section < sections - 1).astype(jnp.int32)
    pl.semaphore_wait(barrier, group - 1 + pipe_peers)

    def halo_copy(to):
        return pltpu.make_async_remote_copy(
            src_ref=halo_out, dst_ref=halo_in, send_sem=halo_sem.at[0], recv_sem=halo_sem.at[1],
            device_id={"seq": to}, device_id_type=MESH,
        )

    @pl.when(seq < shards - 1)
    def _():
        halo_copy(seq + 1).start()

    ext[half:] = normed_bf.astype(f32)
    taps[0] = normed_bf

    @pl.when(seq == 0)
    def _():
        ext[:half] = jnp.zeros((half, width), f32)

    @pl.when(seq > 0)
    def _():
        halo_copy(seq - 1).wait_recv()
        ext[:half] = halo_in[...].astype(f32)

    def shifted(dest, slot, base, way, tap):
        for place in range(sections):
            start = base + way * tap * (rows // 4 >> place)

            @pl.when(section == place)
            def _():
                dest[slot] = ext[start : start + rows].astype(bf16)

    for tap in range(1, KERNEL):
        shifted(taps, tap, half, -1, tap)
    for tap in range(KERNEL):
        part = pl.ds(tap * width, width)
        pltpu.make_async_copy(weight_hbm.at[part], weight_ref.at[part], w_sem.at[tap]).wait()

    info = row_ref[...]
    kinds = table_ref.shape[0]
    ids = jnp.broadcast_to(info[3:4], (kinds, rows)).astype(jnp.int32)
    pick = jnp.where(ids == lax.broadcasted_iota(jnp.int32, (kinds, rows), 0), 1.0, 0.0).astype(f32)
    onehot = jnp.transpose(pick).astype(bf16)

    def forward(i, logits):
        cols = pl.ds(pl.multiple_of(i * BLOCK, BLOCK), BLOCK)
        pre = jnp.dot(onehot, table_ref[:, cols], preferred_element_type=f32)
        for tap in range(KERNEL):
            pre = pre + jnp.dot(
                taps[tap], weight_ref[tap * width : (tap + 1) * width, cols],
                preferred_element_type=f32,
            )
        square = pre * pre
        scale = 0.7978845608028654
        curve = jnp.tanh(scale * (pre + 0.044715 * (square * pre)))
        slope[:, cols] = 0.5 * (1.0 + curve) + 0.5 * pre * (1.0 - curve * curve) * (
            scale * (1.0 + 0.134145 * square)
        )
        out_bf = (x_ref[:, cols].astype(f32) + 0.5 * pre * (1.0 + curve)).astype(bf16)
        return logits + lax.dot_general(
            head_ref[:, cols], out_bf, (((1,), (1,)), ((), ())), preferred_element_type=f32
        )

    logits = lax.fori_loop(0, width // BLOCK, forward, jnp.zeros((8, rows), f32))

    def send_taps():
        block_rows = tap_src.shape[1]
        for tap in range(KERNEL):
            weight_rows = jnp.transpose(taps[tap].astype(f32)).astype(bf16)
            low = tap * width
            while low < (tap + 1) * width:
                peer = low // share
                high = min((peer + 1) * share, (tap + 1) * width)
                tap_src[peer, low - peer * share : high - peer * share] = weight_rows[
                    low - tap * width : high - tap * width
                ]
                low = high
        ids_rows = jnp.broadcast_to(row_ref[3:4], (block_rows - share, rows)).astype(bf16)
        for peer in range(group):
            tap_src[peer, share:] = ids_rows

        @pl.loop(1, group)
        def _(i):
            peer, d, s = peer_id(i)
            pltpu.make_async_remote_copy(
                src_ref=tap_src.at[peer],
                dst_ref=tap_all.at[me],
                send_sem=tap_send.at[peer], recv_sem=tap_recv.at[me],
                device_id={"dp": d, "seq": s}, device_id_type=MESH,
            ).start()
        tap_all[me] = tap_src[me]

    def pipe_copy(to):
        return pltpu.make_async_remote_copy(
            src_ref=gin_buf, dst_ref=inc, send_sem=pipe_sem.at[0], recv_sem=pipe_sem.at[1],
            device_id={"pipe": to}, device_id_type=MESH,
        )

    @pl.when(is_last)
    def _():
        a, b = logits[0:1], logits[1:2]
        y, z, m = info[0:1], info[1:2], info[2:3]
        sa, na = jax.nn.sigmoid(a), jax.nn.sigmoid(-a)
        sb, nb = jax.nn.sigmoid(b), jax.nn.sigmoid(-b)
        rest = (1.0 - z) / (na + sa * nb)
        first = m * ((1.0 - y) * sa - (y + z) * na + rest * (sa * na * sb))
        second = m * (rest * (sa * sb * nb) - z * nb)
        columns = jnp.transpose(
            jnp.concatenate([first, second, jnp.zeros((6, rows), f32)], axis=0)
        )
        heads = head_ref[...].astype(f32)
        gout[...] = columns[:, 0:1] * heads[0:1] + columns[:, 1:2] * heads[1:2]

    @pl.when(section < sections - 1)
    def _():
        send_taps()
        pipe_copy(section + 1).wait_recv()
        gout[...] = inc[...].astype(f32)

    mine = pl.ds(pl.multiple_of(me * rows, rows), rows)
    grad_pre = (gout[...] * slope[...]).astype(bf16)
    gp_all[mine] = grad_pre

    def back_copy(to):
        return pltpu.make_async_remote_copy(
            src_ref=gp_all.at[pl.ds(pl.multiple_of(me * rows, rows), half)], dst_ref=back_in,
            send_sem=back_sem.at[0], recv_sem=back_sem.at[1],
            device_id={"seq": to}, device_id_type=MESH,
        )

    @pl.when(seq > 0)
    def _():
        back_copy(seq - 1).start()

    def dp_copy(source, to):
        piece = gp_all.at[pl.ds(pl.multiple_of((source * shards + seq) * rows, rows), rows)]
        return pltpu.make_async_remote_copy(
            src_ref=piece, dst_ref=piece, send_sem=dp_send.at[to], recv_sem=dp_recv.at[source],
            device_id={"dp": to}, device_id_type=MESH,
        )

    def seq_copy(user, source, to):
        piece = gp_all.at[pl.ds(pl.multiple_of((user * shards + source) * rows, rows), rows)]
        return pltpu.make_async_remote_copy(
            src_ref=piece, dst_ref=piece, send_sem=f_send.at[user, to],
            recv_sem=f_recv.at[user, source], device_id={"seq": to}, device_id_type=MESH,
        )

    @pl.loop(1, users)
    def _(i):
        dp_copy(dp, lax.rem(dp + i, users)).start()

    def times(lhs, tap, first):
        @pl.loop(0, width // BLOCK)
        def _(i):
            cols = pl.ds(pl.multiple_of(i * BLOCK, BLOCK), BLOCK)
            rows_of = pl.ds(pl.multiple_of(tap * width + i * BLOCK, BLOCK), BLOCK)
            value = lax.dot_general(
                lhs[...], weight_ref[rows_of], (((1,), (1,)), ((), ())),
                preferred_element_type=f32,
            )
            gnorm[:, cols] = value if first else gnorm[:, cols] + value

    times(gp_all.at[mine], 0, True)
    ext[:rows] = grad_pre.astype(f32)

    @pl.when(seq == shards - 1)
    def _():
        ext[rows:] = jnp.zeros((half, width), f32)

    @pl.when(seq < shards - 1)
    def _():
        back_copy(seq + 1).wait_recv()
        ext[rows:] = back_in[...].astype(f32)

    for tap in range(1, KERNEL):
        shifted(back, tap - 1, 0, 1, tap)
        times(back.at[tap - 1], tap, False)
    x = x_ref[...].astype(f32)
    inv = lax.rsqrt(jnp.mean(x * x, axis=-1, keepdims=True) + EPS)
    normed = x * inv
    grad_normed = gnorm[...]
    inner = jnp.mean(grad_normed * normed, axis=-1, keepdims=True)
    gin_buf[...] = (gout[...] + inv * (grad_normed - normed * inner)).astype(bf16)

    @pl.when(section > 0)
    def _():
        pipe_copy(section - 1).start()

    gin_ref[...] = gin_buf[...]

    @pl.when(is_last)
    def _():
        send_taps()

    @pl.loop(1, shards)
    def _(i):
        seq_copy(dp, seq, lax.rem(seq + i, shards)).start()

    @pl.loop(1, users)
    def _(i):
        user = lax.rem(dp + i, users)
        dp_copy(user, user).wait_recv()

        @pl.loop(1, shards)
        def _(j):
            seq_copy(user, seq, lax.rem(seq + j, shards)).start()

    @pl.loop(1, group)
    def _(i):
        peer, d, s = peer_id(i)
        pltpu.make_async_remote_copy(
            src_ref=tap_src.at[peer],
            dst_ref=tap_all.at[peer],
            send_sem=tap_send.at[peer], recv_sem=tap_recv.at[peer],
            device_id={"dp": d, "seq": s}, device_id_type=MESH,
        ).wait()

    @pl.loop(0, users)
    def _(user):
        @pl.loop(1, shards)
        def _(j):
            seq_copy(user, lax.rem(seq + j, shards), lax.rem(seq + j, shards)).wait()

    kind = me * kind_share + lax.broadcasted_iota(
        jnp.int32, (tap_src.shape[1] - share, rows), 0
    )
    conv_ref[...] = jnp.zeros_like(conv_ref)
    type_ref[...] = jnp.zeros_like(type_ref)

    @pl.loop(0, users)
    def _(user):
        pieces = [tap_all[user * shards + s] for s in range(shards)]
        left = jnp.concatenate([piece[:share] for piece in pieces], axis=1)
        picks = jnp.concatenate(
            [
                jnp.where(piece[share:].astype(f32).astype(jnp.int32) == kind, 1.0, 0.0).astype(bf16)
                for piece in pieces
            ],
            axis=1,
        )
        span = pl.ds(pl.multiple_of(user * shards * rows, shards * rows), shards * rows)
        for i in range(width // BLOCK):
            cols = slice(i * BLOCK, (i + 1) * BLOCK)
            right = gp_all[span, cols]
            conv_ref[:, cols] += jnp.dot(left, right, preferred_element_type=f32)
            type_ref[:, cols] += jnp.dot(picks, right, preferred_element_type=f32)[:kind_share]

    @pl.loop(1, users)
    def _(i):
        dp_copy(dp, lax.rem(dp + i, users)).wait_send()

    @pl.when(section > 0)
    def _():
        pipe_copy(section - 1).wait_send()

    @pl.when(seq > 0)
    def _():
        back_copy(seq - 1).wait_send()

    @pl.when(seq < shards - 1)
    def _():
        halo_copy(seq + 1).wait_send()


def on_device(
    section_input, event_ids, lengths, clicks, conversions, conv_weight, type_table, head_weight
):
    inputs_bf = section_input[0, 0]
    rows, width = inputs_bf.shape
    half = rows // 2
    kinds = type_table.shape[1]
    users, shards, sections = (lax.axis_size(name) for name in ("dp", "seq", "pipe"))
    group = users * shards
    share = KERNEL * width // group
    kind_share = kinds // group
    block_rows = share + -(-kind_share // 16) * 16
    position = lax.axis_index("seq") * rows + jnp.arange(rows, dtype=jnp.int32)
    label = clicks[0].astype(jnp.float32)
    lines = jnp.stack(
        [
            label,
            label * conversions[0].astype(jnp.float32),
            (position < lengths[0]).astype(jnp.float32),
            event_ids[0].astype(jnp.float32),
        ]
    )
    lines = jnp.pad(lines, ((0, 4), (0, 0)))
    heads = jnp.pad(head_weight, ((0, 6), (0, 0)))
    vmem = pl.BlockSpec(memory_space=pltpu.VMEM)
    dma = pltpu.SemaphoreType.DMA
    f32, bf16 = jnp.float32, jnp.bfloat16
    conv, kind, grad_in = pl.pallas_call(
        functools.partial(kernel, users, shards, sections, kind_share),
        out_shape=(
            jax.ShapeDtypeStruct((share, width), f32),
            jax.ShapeDtypeStruct((kind_share, width), f32),
            jax.ShapeDtypeStruct((rows, width), bf16),
        ),
        in_specs=[vmem, vmem, pl.BlockSpec(memory_space=pl.ANY), vmem, vmem],
        out_specs=(vmem, vmem, vmem),
        scratch_shapes=[
            pltpu.VMEM((KERNEL * width, width), bf16),
            pltpu.VMEM((rows + half, width), f32),
            pltpu.VMEM((KERNEL, rows, width), bf16),
            pltpu.VMEM((KERNEL - 1, rows, width), bf16),
            pltpu.VMEM((group, block_rows, rows), bf16),
            pltpu.VMEM((group, block_rows, rows), bf16),
            pltpu.VMEM((rows, width), f32),
            pltpu.VMEM((rows, width), f32),
            pltpu.VMEM((rows, width), f32),
            pltpu.VMEM((group * rows, width), bf16),
            pltpu.VMEM((half, width), bf16),
            pltpu.VMEM((half, width), bf16),
            pltpu.VMEM((half, width), bf16),
            pltpu.VMEM((rows, width), bf16),
            pltpu.VMEM((rows, width), bf16),
            dma((KERNEL,)),
            dma((2,)),
            dma((2,)),
            dma((2,)),
            dma((group,)),
            dma((group,)),
            dma((users,)),
            dma((users,)),
            dma((users, shards)),
            dma((users, shards)),
        ],
        compiler_params=pltpu.CompilerParams(
            collective_id=0, has_side_effects=True, vmem_limit_bytes=56 * 1024 * 1024
        ),
    )(inputs_bf, lines, conv_weight[0], type_table[0], heads)
    return (conv[None], kind[None], grad_in[None, None])


def solution(mesh):
    placed = (
        P("pipe", "dp", "seq", None),
        P("dp", "seq"),
        P("dp"),
        P("dp", "seq"),
        P("dp", "seq"),
        P("pipe", None, None),
        P("pipe", None, None),
        P(),
    )
    return jax.shard_map(
        on_device,
        mesh=mesh,
        in_specs=placed,
        out_specs=(
            P("pipe", ("dp", "seq"), None),
            P("pipe", ("dp", "seq"), None),
            P("pipe", "dp", "seq", None),
        ),
        check_vma=False,
    )
```

time: 122 us -> 81.3 us (0.67)
  the two profiles are of different devices: /device:TPU:0 before, /device:TPU:25 now
where the time goes in v2:
time: 81.3 us; the launch traced here: 81 us
  Pallas kernels  71.7 us (88%)
  local copies, waits for them, and re-layouts  5.39 us (7%)
  other arithmetic  2.6 us (3%)
  between operations  1.31 us (2%)
    pallas_call x1, Pallas kernels, on_device(): pl.pallas_call(functools.partial(kernel, users, shards, sections, kind_sh...  71.7 us
    unnamed x7, local copies, waits for them, and re-layouts  4.1 us

profile of v2, /device:TPU:25, one launch (start us, length us, event | category | flops | bytes accessed | tf_op | source)
XLA Modules:
  0.0 81.0 jit_solution(16927168368460426747)
XLA Ops:
  1.3 0.7 convert_element_type.30
  2.0 0.7 convert_multiply_fusion
  2.6 0.7 convert_element_type.27
  3.3 0.6 select_maximum_fusion.row_ref
  3.9 1.3 %pad.9.head_ref = bf16[8,1024]{1,0:T(8,128)(2,1)} pad(bf16[2,1024]{1,0:T(2,128)(2,1)} %param.15, bf16[]{:T(256)} %constant.10.clone.1), padding=0_6x0_0 | pad | bytes 20482 | tf_op jit(solution)/shard_map/jit(_pad)/pad | solution.py:351
  5.2 71.7 %shard_map.103 = (f32[384,1024]{1,0:T(8,128)}, f32[8,1024]{1,0:T(8,128)}, bf16[128,1024]{1,0:T(8,128)(2,1)}) custom-call(bf16[128,1024]{1,0:T(8,128)(2,1)} %bitcast.10, f32[8,128]{1,0:T(8,128)} %select_maximum_fusion.row_ref, bf16[3072,1024]{1,0:T(8,128)(2,1)} %bitcast.8, bf16[64,1024]{1,0:T(8,128)(2,1)} %bitcast.12, bf16[8,1024]{1,0:T(8,128)(2,1)} %pad.9.head_ref), custom_call_target="tpu_custom_call" | custom-call | tf_op jit(solution)/shard_map/pallas_call | solution.py:355
  76.9 0.0 copy-start.1
  76.9 0.0 copy-start
  76.9 2.8 %copy.15 = f32[1,384,1024]{2,1,0:T(8,128)} copy(f32[1,384,1024]{2,1,0:T(8,128)} %bitcast.9) | data formatting | bytes 3145728
  79.7 0.0 copy-done.1
  79.7 0.6 copy.16
  80.3 0.0 copy-done
  80.3 0.7 copy.17
  (1 shorter events, 0.0 us)
Async XLA Ops:
  76.9 2.8 %copy-start.1 = (f32[8,1024]{1,0:T(8,128)S(1)}, f32[8,1024]{1,0:T(8,128)}, u32[]{:S(2)}) copy-start(f32[8,1024]{1,0:T(8,128)} %get-tuple-element.7) | copy-start | bytes 98308
  76.9 3.4 %copy-start = (bf16[128,1024]{1,0:T(8,128)(2,1)S(1)}, bf16[128,1024]{1,0:T(8,128)(2,1)}, u32[]{:S(2)}) copy-start(bf16[128,1024]{1,0:T(8,128)(2,1)} %get-tuple-element.8) | copy-start | bytes 786436

commit v3 on v2

--- a/solution.py
+++ b/solution.py
@@ -15,10 +15,10 @@
 
 def kernel(
     users, shards, sections, kind_share,
-    x_ref, row_ref, weight_hbm, table_ref, head_ref,
+    x_ref, id_ref, click_ref, convert_ref, length_ref, weight_hbm, table_ref, head_ref,
     conv_ref, type_ref, gin_ref,
     weight_ref, ext, taps, back, tap_src, tap_all, slope, gnorm, gout, gp_all, halo_out, halo_in,
-    back_in, inc, gin_buf,
+    back_in, inc, gin_buf, heads,
     w_sem, halo_sem, back_sem, pipe_sem, tap_send, tap_recv, dp_send, dp_recv, f_send, f_recv,
 ):
     rows, width = x_ref.shape
@@ -98,9 +98,12 @@
         part = pl.ds(tap * width, width)
         pltpu.make_async_copy(weight_hbm.at[part], weight_ref.at[part], w_sem.at[tap]).wait()
 
-    info = row_ref[...]
+    id_row = id_ref[...]
+    heads[...] = jnp.concatenate(
+        [head_ref[...].astype(f32), jnp.zeros((6, width), f32)], axis=0
+    )
     kinds = table_ref.shape[0]
-    ids = jnp.broadcast_to(info[3:4], (kinds, rows)).astype(jnp.int32)
+    ids = jnp.broadcast_to(id_row, (kinds, rows))
     pick = jnp.where(ids == lax.broadcasted_iota(jnp.int32, (kinds, rows), 0), 1.0, 0.0).astype(f32)
     onehot = jnp.transpose(pick).astype(bf16)
 
@@ -120,7 +123,7 @@
         )
         out_bf = (x_ref[:, cols].astype(f32) + 0.5 * pre * (1.0 + curve)).astype(bf16)
         return logits + lax.dot_general(
-            head_ref[:, cols], out_bf, (((1,), (1,)), ((), ())), preferred_element_type=f32
+            heads[:, cols].astype(bf16), out_bf, (((1,), (1,)), ((), ())), preferred_element_type=f32
         )
 
     logits = lax.fori_loop(0, width // BLOCK, forward, jnp.zeros((8, rows), f32))
@@ -137,7 +140,7 @@
                     low - tap * width : high - tap * width
                 ]
                 low = high
-        ids_rows = jnp.broadcast_to(row_ref[3:4], (block_rows - share, rows)).astype(bf16)
+        ids_rows = jnp.broadcast_to(id_row.astype(f32), (block_rows - share, rows)).astype(bf16)
         for peer in range(group):
             tap_src[peer, share:] = ids_rows
 
@@ -161,7 +164,10 @@
     @pl.when(is_last)
     def _():
         a, b = logits[0:1], logits[1:2]
-        y, z, m = info[0:1], info[1:2], info[2:3]
+        y = click_ref[...].astype(f32)
+        z = y * convert_ref[...].astype(f32)
+        position = seq * rows + lax.broadcasted_iota(jnp.int32, (1, rows), 1)
+        m = jnp.where(position < length_ref[0], 1.0, 0.0).astype(f32)
         sa, na = jax.nn.sigmoid(a), jax.nn.sigmoid(-a)
         sb, nb = jax.nn.sigmoid(b), jax.nn.sigmoid(-b)
         rest = (1.0 - z) / (na + sa * nb)
@@ -170,7 +176,6 @@
         columns = jnp.transpose(
             jnp.concatenate([first, second, jnp.zeros((6, rows), f32)], axis=0)
         )
-        heads = head_ref[...].astype(f32)
         gout[...] = columns[:, 0:1] * heads[0:1] + columns[:, 1:2] * heads[1:2]
 
     @pl.when(section < sections - 1)
@@ -194,12 +199,25 @@
     def _():
         back_copy(seq - 1).start()
 
-    def dp_copy(source, to):
+    def line_copy(source, to, way):
         piece = gp_all.at[pl.ds(pl.multiple_of((source * shards + seq) * rows, rows), rows)]
         return pltpu.make_async_remote_copy(
-            src_ref=piece, dst_ref=piece, send_sem=dp_send.at[to], recv_sem=dp_recv.at[source],
-            device_id={"dp": to}, device_id_type=MESH,
-        )
+            src_ref=piece, dst_ref=piece, send_sem=dp_send.at[source, way],
+            recv_sem=dp_recv.at[source], device_id={"dp": to}, device_id_type=MESH,
+        )
+
+    def pass_on(source, left, right):
+        if left:
+
+            @pl.when(dp > 0)
+            def _():
+                line_copy(source, dp - 1, 0).start()
+
+        if right:
+
+            @pl.when(dp < users - 1)
+            def _():
+                line_copy(source, dp + 1, 1).start()
 
     def seq_copy(user, source, to):
         piece = gp_all.at[pl.ds(pl.multiple_of((user * shards + source) * rows, rows), rows)]
@@ -208,9 +226,7 @@
             recv_sem=f_recv.at[user, source], device_id={"seq": to}, device_id_type=MESH,
         )
 
-    @pl.loop(1, users)
-    def _(i):
-        dp_copy(dp, lax.rem(dp + i, users)).start()
+    pass_on(dp, True, True)
 
     def times(lhs, tap, first):
         @pl.loop(0, width // BLOCK)
@@ -255,18 +271,14 @@
     def _():
         send_taps()
 
-    @pl.loop(1, shards)
-    def _(i):
-        seq_copy(dp, seq, lax.rem(seq + i, shards)).start()
-
-    @pl.loop(1, users)
-    def _(i):
-        user = lax.rem(dp + i, users)
-        dp_copy(user, user).wait_recv()
-
+    def share_out(user):
         @pl.loop(1, shards)
         def _(j):
             seq_copy(user, seq, lax.rem(seq + j, shards)).start()
+
+    share_out(dp)
+    conv_ref[...] = jnp.zeros_like(conv_ref)
+    type_ref[...] = jnp.zeros_like(type_ref)
 
     @pl.loop(1, group)
     def _(i):
@@ -278,20 +290,16 @@
             device_id={"dp": d, "seq": s}, device_id_type=MESH,
         ).wait()
 
-    @pl.loop(0, users)
-    def _(user):
-        @pl.loop(1, shards)
-        def _(j):
-            seq_copy(user, lax.rem(seq + j, shards), lax.rem(seq + j, shards)).wait()
-
     kind = me * kind_share + lax.broadcasted_iota(
         jnp.int32, (tap_src.shape[1] - share, rows), 0
     )
-    conv_ref[...] = jnp.zeros_like(conv_ref)
-    type_ref[...] = jnp.zeros_like(type_ref)
-
-    @pl.loop(0, users)
-    def _(user):
+
+    def multiply(user):
+        @pl.loop(1, shards)
+        def _(j):
+            other = lax.rem(seq + j, shards)
+            seq_copy(user, other, other).wait()
+
         pieces = [tap_all[user * shards + s] for s in range(shards)]
         left = jnp.concatenate([piece[:share] for piece in pieces], axis=1)
         picks = jnp.concatenate(
@@ -308,9 +316,39 @@
             conv_ref[:, cols] += jnp.dot(left, right, preferred_element_type=f32)
             type_ref[:, cols] += jnp.dot(picks, right, preferred_element_type=f32)[:kind_share]
 
-    @pl.loop(1, users)
-    def _(i):
-        dp_copy(dp, lax.rem(dp + i, users)).wait_send()
+    @pl.loop(0, users)
+    def _(h):
+        before, after = dp - h - 1, dp + h + 1
+
+        @pl.when(before >= 0)
+        def _():
+            line_copy(before, before, 1).wait_recv()
+            pass_on(before, False, True)
+            share_out(before)
+
+        @pl.when(after < users)
+        def _():
+            line_copy(after, after, 0).wait_recv()
+            pass_on(after, True, False)
+            share_out(after)
+
+        @pl.when(dp - h >= 0)
+        def _():
+            multiply(dp - h)
+
+        @pl.when((h > 0) & (dp + h < users))
+        def _():
+            multiply(dp + h)
+
+    @pl.loop(0, users)
+    def _(source):
+        @pl.when((source >= dp) & (dp > 0))
+        def _():
+            line_copy(source, dp - 1, 0).wait_send()
+
+        @pl.when((source <= dp) & (dp < users - 1))
+        def _():
+            line_copy(source, dp + 1, 1).wait_send()
 
     @pl.when(section > 0)
     def _():
@@ -337,18 +375,6 @@
     share = KERNEL * width // group
     kind_share = kinds // group
     block_rows = share + -(-kind_share // 16) * 16
-    position = lax.axis_index("seq") * rows + jnp.arange(rows, dtype=jnp.int32)
-    label = clicks[0].astype(jnp.float32)
-    lines = jnp.stack(
-        [
-            label,
-            label * conversions[0].astype(jnp.float32),
-            (position < lengths[0]).astype(jnp.float32),
-            event_ids[0].astype(jnp.float32),
-        ]
-    )
-    lines = jnp.pad(lines, ((0, 4), (0, 0)))
-    heads = jnp.pad(head_weight, ((0, 6), (0, 0)))
     vmem = pl.BlockSpec(memory_space=pltpu.VMEM)
     dma = pltpu.SemaphoreType.DMA
     f32, bf16 = jnp.float32, jnp.bfloat16
@@ -359,7 +385,10 @@
             jax.ShapeDtypeStruct((kind_share, width), f32),
             jax.ShapeDtypeStruct((rows, width), bf16),
         ),
-        in_specs=[vmem, vmem, pl.BlockSpec(memory_space=pl.ANY), vmem, vmem],
+        in_specs=[
+            vmem, vmem, vmem, vmem, pl.BlockSpec(memory_space=pltpu.SMEM),
+            pl.BlockSpec(memory_space=pl.ANY), vmem, vmem,
+        ],
         out_specs=(vmem, vmem, vmem),
         scratch_shapes=[
             pltpu.VMEM((KERNEL * width, width), bf16),
@@ -377,13 +406,14 @@
             pltpu.VMEM((half, width), bf16),
             pltpu.VMEM((rows, width), bf16),
             pltpu.VMEM((rows, width), bf16),
+            pltpu.VMEM((8, width), f32),
             dma((KERNEL,)),
             dma((2,)),
             dma((2,)),
             dma((2,)),
             dma((group,)),
             dma((group,)),
-            dma((users,)),
+            dma((users, 2)),
             dma((users,)),
             dma((users, shards)),
             dma((users, shards)),
@@ -391,7 +421,10 @@
         compiler_params=pltpu.CompilerParams(
             collective_id=0, has_side_effects=True, vmem_limit_bytes=56 * 1024 * 1024
         ),
-    )(inputs_bf, lines, conv_weight[0], type_table[0], heads)
+    )(
+        inputs_bf, event_ids, clicks, conversions, lengths, conv_weight[0], type_table[0],
+        head_weight,
+    )
     return (conv[None], kind[None], grad_in[None, None])
 
 

time: 81.3 us -> 72.2 us (0.89)
  the two profiles are of different devices: /device:TPU:25 before, /device:TPU:0 now
where the time goes in v3:
time: 72.2 us; the launch traced here: 72.1 us
  Pallas kernels  66.7 us (92%)
  local copies, waits for them, and re-layouts  4.1 us (6%)
  between operations  1.3 us (2%)
    pallas_call x1, Pallas kernels, on_device(): pl.pallas_call(functools.partial(kernel, users, shards, sections, kind_sh...  66.7 us
    unnamed x7, local copies, waits for them, and re-layouts  4.1 us

profile of v3, /device:TPU:0, one launch (start us, length us, event | category | flops | bytes accessed | tf_op | source)
XLA Modules:
  0.0 72.1 jit_solution(11466561203642270777)
XLA Ops:
  1.3 66.7 %shard_map.103 = (f32[384,1024]{1,0:T(8,128)}, f32[8,1024]{1,0:T(8,128)}, bf16[128,1024]{1,0:T(8,128)(2,1)}) custom-call(bf16[128,1024]{1,0:T(8,128)(2,1)} %bitcast.9, s32[1,128]{1,0:T(1,128)} %id_ref.1, s32[1,128]{1,0:T(1,128)} %click_ref.1, s32[1,128]{1,0:T(1,128)} %convert_ref.1, s32[1]{0:T(128)S(6)} %copy.14.length_ref, bf16[3072,1024]{1,0:T(8,128)(2,1)} %bitcast.6, ...), custom_call_target="tpu_custom_call" | custom-call | tf_op jit(solution)/shard_map/pallas_call | solution.py:381
  68.0 0.0 copy-start.1
  68.0 0.0 copy-start
  68.0 2.8 %copy.15 = f32[1,384,1024]{2,1,0:T(8,128)} copy(f32[1,384,1024]{2,1,0:T(8,128)} %bitcast.7) | data formatting | bytes 3145728
  70.7 0.0 copy-done.1
  70.7 0.6 copy.16
  71.4 0.0 copy-done
  71.4 0.7 copy.17
Async XLA Ops:
  68.0 2.8 %copy-start.1 = (f32[8,1024]{1,0:T(8,128)S(1)}, f32[8,1024]{1,0:T(8,128)}, u32[]{:S(2)}) copy-start(f32[8,1024]{1,0:T(8,128)} %get-tuple-element.7) | copy-start | bytes 98308
  68.0 3.4 %copy-start = (bf16[128,1024]{1,0:T(8,128)(2,1)S(1)}, bf16[128,1024]{1,0:T(8,128)(2,1)}, u32[]{:S(2)}) copy-start(bf16[128,1024]{1,0:T(8,128)(2,1)} %get-tuple-element.8) | copy-start | bytes 786436

commit v4 on v3

--- a/solution.py
+++ b/solution.py
@@ -84,13 +84,13 @@
         halo_copy(seq - 1).wait_recv()
         ext[:half] = halo_in[...].astype(f32)
 
-    def shifted(dest, slot, base, way, tap):
+    def shifted(dest, slot, base, way, tap, cols=slice(None)):
         for place in range(sections):
             start = base + way * tap * (rows // 4 >> place)
 
             @pl.when(section == place)
             def _():
-                dest[slot] = ext[start : start + rows].astype(bf16)
+                dest[slot, :, cols] = ext[start : start + rows, cols].astype(bf16)
 
     for tap in range(1, KERNEL):
         shifted(taps, tap, half, -1, tap)
@@ -155,9 +155,13 @@
             ).start()
         tap_all[me] = tap_src[me]
 
-    def pipe_copy(to):
+    chunks = width // BLOCK
+
+    def pipe_copy(to, c):
+        cols = pl.ds(c * BLOCK, BLOCK)
         return pltpu.make_async_remote_copy(
-            src_ref=gin_buf, dst_ref=inc, send_sem=pipe_sem.at[0], recv_sem=pipe_sem.at[1],
+            src_ref=gin_buf.at[:, cols], dst_ref=inc.at[:, cols],
+            send_sem=pipe_sem.at[0, c], recv_sem=pipe_sem.at[1, c],
             device_id={"pipe": to}, device_id_type=MESH,
         )
 
@@ -181,23 +185,17 @@
     @pl.when(section < sections - 1)
     def _():
         send_taps()
-        pipe_copy(section + 1).wait_recv()
-        gout[...] = inc[...].astype(f32)
 
     mine = pl.ds(pl.multiple_of(me * rows, rows), rows)
-    grad_pre = (gout[...] * slope[...]).astype(bf16)
-    gp_all[mine] = grad_pre
-
-    def back_copy(to):
+
+    def back_copy(to, c):
+        cols = pl.ds(c * BLOCK, BLOCK)
         return pltpu.make_async_remote_copy(
-            src_ref=gp_all.at[pl.ds(pl.multiple_of(me * rows, rows), half)], dst_ref=back_in,
-            send_sem=back_sem.at[0], recv_sem=back_sem.at[1],
+            src_ref=gp_all.at[pl.ds(pl.multiple_of(me * rows, rows), half), cols],
+            dst_ref=back_in.at[:, cols],
+            send_sem=back_sem.at[0, c], recv_sem=back_sem.at[1, c],
             device_id={"seq": to}, device_id_type=MESH,
         )
-
-    @pl.when(seq > 0)
-    def _():
-        back_copy(seq - 1).start()
 
     def line_copy(source, to, way):
         piece = gp_all.at[pl.ds(pl.multiple_of((source * shards + seq) * rows, rows), rows)]
@@ -226,44 +224,71 @@
             recv_sem=f_recv.at[user, source], device_id={"seq": to}, device_id_type=MESH,
         )
 
-    pass_on(dp, True, True)
-
-    def times(lhs, tap, first):
-        @pl.loop(0, width // BLOCK)
-        def _(i):
-            cols = pl.ds(pl.multiple_of(i * BLOCK, BLOCK), BLOCK)
-            rows_of = pl.ds(pl.multiple_of(tap * width + i * BLOCK, BLOCK), BLOCK)
+    def times(lhs, tap, c):
+        for i in range(chunks):
+            out = slice(i * BLOCK, (i + 1) * BLOCK)
+            low = tap * width + i * BLOCK
             value = lax.dot_general(
-                lhs[...], weight_ref[rows_of], (((1,), (1,)), ((), ())),
-                preferred_element_type=f32,
+                lhs, weight_ref[low : low + BLOCK, c * BLOCK : (c + 1) * BLOCK],
+                (((1,), (1,)), ((), ())), preferred_element_type=f32,
             )
-            gnorm[:, cols] = value if first else gnorm[:, cols] + value
-
-    times(gp_all.at[mine], 0, True)
-    ext[:rows] = grad_pre.astype(f32)
+            if tap == 0 and c == 0:
+                gnorm[:, out] = value
+            else:
+                gnorm[:, out] += value
+
+    def later_taps(c):
+        cols = slice(c * BLOCK, (c + 1) * BLOCK)
+
+        @pl.when(seq < shards - 1)
+        def _():
+            back_copy(seq + 1, c).wait_recv()
+            ext[rows:, cols] = back_in[:, cols].astype(f32)
+
+        for tap in range(1, KERNEL):
+            shifted(back, tap - 1, 0, 1, tap, cols)
+            times(back[tap - 1, :, cols], tap, c)
 
     @pl.when(seq == shards - 1)
     def _():
         ext[rows:] = jnp.zeros((half, width), f32)
 
-    @pl.when(seq < shards - 1)
-    def _():
-        back_copy(seq + 1).wait_recv()
-        ext[rows:] = back_in[...].astype(f32)
-
-    for tap in range(1, KERNEL):
-        shifted(back, tap - 1, 0, 1, tap)
-        times(back.at[tap - 1], tap, False)
+    for c in range(chunks):
+        cols = slice(c * BLOCK, (c + 1) * BLOCK)
+
+        @pl.when(section < sections - 1)
+        def _():
+            pipe_copy(section + 1, c).wait_recv()
+            gout[:, cols] = inc[:, cols].astype(f32)
+
+        grad_pre = (gout[:, cols] * slope[:, cols]).astype(bf16)
+        gp_all[mine, cols] = grad_pre
+
+        @pl.when(seq > 0)
+        def _():
+            back_copy(seq - 1, c).start()
+
+        if c == chunks - 1:
+            pass_on(dp, True, True)
+        ext[:rows, cols] = grad_pre.astype(f32)
+        times(grad_pre, 0, c)
+        if c > 0:
+            later_taps(c - 1)
+    later_taps(chunks - 1)
     x = x_ref[...].astype(f32)
     inv = lax.rsqrt(jnp.mean(x * x, axis=-1, keepdims=True) + EPS)
     normed = x * inv
     grad_normed = gnorm[...]
     inner = jnp.mean(grad_normed * normed, axis=-1, keepdims=True)
-    gin_buf[...] = (gout[...] + inv * (grad_normed - normed * inner)).astype(bf16)
-
-    @pl.when(section > 0)
-    def _():
-        pipe_copy(section - 1).start()
+    for c in range(chunks):
+        cols = slice(c * BLOCK, (c + 1) * BLOCK)
+        gin_buf[:, cols] = (
+            gout[:, cols] + inv * (grad_normed[:, cols] - normed[:, cols] * inner)
+        ).astype(bf16)
+
+        @pl.when(section > 0)
+        def _():
+            pipe_copy(section - 1, c).start()
 
     gin_ref[...] = gin_buf[...]
 
@@ -352,11 +377,13 @@
 
     @pl.when(section > 0)
     def _():
-        pipe_copy(section - 1).wait_send()
+        for c in range(chunks):
+            pipe_copy(section - 1, c).wait_send()
 
     @pl.when(seq > 0)
     def _():
-        back_copy(seq - 1).wait_send()
+        for c in range(chunks):
+            back_copy(seq - 1, c).wait_send()
 
     @pl.when(seq < shards - 1)
     def _():
@@ -387,7 +414,7 @@
         ),
         in_specs=[
             vmem, vmem, vmem, vmem, pl.BlockSpec(memory_space=pltpu.SMEM),
-            pl.BlockSpec(memory_space=pl.ANY), vmem, vmem,
+            pl.BlockSpec(memory_space=pltpu.HBM), vmem, vmem,
         ],
         out_specs=(vmem, vmem, vmem),
         scratch_shapes=[
@@ -409,8 +436,8 @@
             pltpu.VMEM((8, width), f32),
             dma((KERNEL,)),
             dma((2,)),
-            dma((2,)),
-            dma((2,)),
+            dma((2, width // BLOCK)),
+            dma((2, width // BLOCK)),
             dma((group,)),
             dma((group,)),
             dma((users, 2)),
@@ -419,7 +446,7 @@
             dma((users, shards)),
         ],
         compiler_params=pltpu.CompilerParams(
-            collective_id=0, has_side_effects=True, vmem_limit_bytes=56 * 1024 * 1024
+            collective_id=0, has_side_effects=True, vmem_limit_bytes=58 * 1024 * 1024
         ),
     )(
         inputs_bf, event_ids, clicks, conversions, lengths, conv_weight[0], type_table[0],

time: 72.2 us -> 62.7 us (0.87)
  Pallas kernels: 66.7 us -> 57.2 us
    pallas_call x1, Pallas kernels: 66.7 us -> 57.2 us  [on_device(): pl.pallas_call(functools.partial(kernel, users, shards, sections, kind_sh...]
where the time goes in v4:
time: 62.7 us; the launch traced here: 62.6 us
  Pallas kernels  57.2 us (91%)
  local copies, waits for them, and re-layouts  4.1 us (7%)
  between operations  1.3 us (2%)
    pallas_call x1, Pallas kernels, on_device(): pl.pallas_call(functools.partial(kernel, users, shards, sections, kind_sh...  57.2 us
    unnamed x7, local copies, waits for them, and re-layouts  4.1 us

profile of v4, /device:TPU:0, one launch (start us, length us, event | category | flops | bytes accessed | tf_op | source)
XLA Modules:
  0.0 62.6 jit_solution(4600231560188990896)
XLA Ops:
  1.3 57.2 %shard_map.103 = (f32[384,1024]{1,0:T(8,128)}, f32[8,1024]{1,0:T(8,128)}, bf16[128,1024]{1,0:T(8,128)(2,1)}) custom-call(bf16[128,1024]{1,0:T(8,128)(2,1)} %bitcast.9, s32[1,128]{1,0:T(1,128)} %id_ref.1, s32[1,128]{1,0:T(1,128)} %click_ref.1, s32[1,128]{1,0:T(1,128)} %convert_ref.1, s32[1]{0:T(128)S(6)} %copy.14.length_ref, bf16[3072,1024]{1,0:T(8,128)(2,1)} %bitcast.6, ...), custom_call_target="tpu_custom_call" | custom-call | tf_op jit(solution)/shard_map/pallas_call | solution.py:408
  58.4 0.0 copy-start.1
  58.5 0.0 copy-start
  58.5 2.8 %copy.15 = f32[1,384,1024]{2,1,0:T(8,128)} copy(f32[1,384,1024]{2,1,0:T(8,128)} %bitcast.7) | data formatting | bytes 3145728
  61.2 0.0 copy-done.1
  61.2 0.6 copy.16
  61.9 0.0 copy-done
  61.9 0.7 %copy.17 = bf16[1,1,128,1024]{3,2,1,0:T(8,128)(2,1)} copy(bf16[1,1,128,1024]{3,2,1,0:T(8,128)(2,1)S(1)} %bitcast.8) | data formatting | bytes 524288
Async XLA Ops:
  58.4 2.8 %copy-start.1 = (f32[8,1024]{1,0:T(8,128)S(1)}, f32[8,1024]{1,0:T(8,128)}, u32[]{:S(2)}) copy-start(f32[8,1024]{1,0:T(8,128)} %get-tuple-element.7) | copy-start | bytes 98308
  58.5 3.4 %copy-start = (bf16[128,1024]{1,0:T(8,128)(2,1)S(1)}, bf16[128,1024]{1,0:T(8,128)(2,1)}, u32[]{:S(2)}) copy-start(bf16[128,1024]{1,0:T(8,128)(2,1)} %get-tuple-element.8) | copy-start | bytes 786436

commit v5 on v4

--- a/solution.py
+++ b/solution.py
@@ -446,7 +446,7 @@
             dma((users, shards)),
         ],
         compiler_params=pltpu.CompilerParams(
-            collective_id=0, has_side_effects=True, vmem_limit_bytes=58 * 1024 * 1024
+            collective_id=0, has_side_effects=True, vmem_limit_bytes=46 * 1024 * 1024
         ),
     )(
         inputs_bf, event_ids, clicks, conversions, lengths, conv_weight[0], type_table[0],

time: 62.7 us -> 63.2 us (level)
  local copies, waits for them, and re-layouts: 4.1 us -> 6.96 us
  Pallas kernels: 57.2 us -> 54.7 us
    unnamed x7 -> x15, local copies, waits for them, and re-layouts: 4.1 us -> 6.96 us
    pallas_call x1, Pallas kernels: 57.2 us -> 54.7 us  [on_device(): pl.pallas_call(functools.partial(kernel, users, shards, sections, kind_sh...]
where the time goes in v5:
time: 63.2 us; the launch traced here: 63 us
  Pallas kernels  54.7 us (87%)
  local copies, waits for them, and re-layouts  6.96 us (11%)
  between operations  1.3 us (2%)
    pallas_call x1, Pallas kernels, on_device(): pl.pallas_call(functools.partial(kernel, users, shards, sections, kind_sh...  54.7 us
    unnamed x15, local copies, waits for them, and re-layouts  6.96 us

profile of v5, /device:TPU:0, one launch (start us, length us, event | category | flops | bytes accessed | tf_op | source)
XLA Modules:
  0.0 63.0 jit_solution(16171750696520575688)
XLA Ops:
  1.3 0.0 copy-start
  1.3 0.9 %copy-done = bf16[1,1,128,1024]{3,2,1,0:T(8,128)(2,1)S(1)} copy-done((bf16[1,1,128,1024]{3,2,1,0:T(8,128)(2,1)S(1)}, bf16[1,1,128,1024]{3,2,1,0:T(8,128)(2,1)}, u32[]{:S(2)}) %copy-start) | copy-done | bytes 262168
  2.2 0.0 copy-start.1
  2.2 0.9 %copy-done.1 = bf16[1,64,1024]{2,1,0:T(8,128)(2,1)S(1)} copy-done((bf16[1,64,1024]{2,1,0:T(8,128)(2,1)S(1)}, bf16[1,64,1024]{2,1,0:T(8,128)(2,1)}, u32[]{:S(2)}) %copy-start.1) | copy-done | bytes 131096
  3.1 0.0 copy-start.2
  3.1 0.7 %copy-done.2 = bf16[2,1024]{1,0:T(2,128)(2,1)S(1)} copy-done((bf16[2,1024]{1,0:T(2,128)(2,1)S(1)}, bf16[2,1024]{1,0:T(2,128)(2,1)}, u32[]{:S(2)}) %copy-start.2) | copy-done | bytes 4120
  3.8 0.0 copy-start.3
  3.8 0.7 %copy-done.3 = s32[1,128]{1,0:T(1,128)S(1)} copy-done((s32[1,128]{1,0:T(1,128)S(1)}, s32[1,128]{1,0:T(1,128)}, u32[]{:S(2)}) %copy-start.3) | copy-done | bytes 536
  4.5 0.0 copy-start.4
  4.5 0.7 %copy-done.4 = s32[1,128]{1,0:T(1,128)S(1)} copy-done((s32[1,128]{1,0:T(1,128)S(1)}, s32[1,128]{1,0:T(1,128)}, u32[]{:S(2)}) %copy-start.4) | copy-done | bytes 536
  5.1 0.0 copy-start.5
  5.1 0.7 %copy-done.5 = s32[1,128]{1,0:T(1,128)S(1)} copy-done((s32[1,128]{1,0:T(1,128)S(1)}, s32[1,128]{1,0:T(1,128)}, u32[]{:S(2)}) %copy-start.5) | copy-done | bytes 536
  5.8 54.7 %shard_map.103 = (f32[384,1024]{1,0:T(8,128)S(1)}, f32[8,1024]{1,0:T(8,128)S(1)}, bf16[128,1024]{1,0:T(8,128)(2,1)S(1)}) custom-call(bf16[128,1024]{1,0:T(8,128)(2,1)S(1)} %bitcast.8, s32[1,128]{1,0:T(1,128)S(1)} %copy-done.3, s32[1,128]{1,0:T(1,128)S(1)} %copy-done.4, s32[1,128]{1,0:T(1,128)S(1)} %copy-done.5, s32[1]{0:T(128)S(6)} %copy.14.length_ref, ...), custom_call_target="tpu_custom_call" | custom-call | tf_op jit(solution)/shard_map/pallas_call | solution.py:408
  60.5 1.1 %copy.15 = f32[1,384,1024]{2,1,0:T(8,128)} copy(f32[1,384,1024]{2,1,0:T(8,128)S(1)} %bitcast.6) | data formatting | bytes 3145728
  61.7 0.6 copy.16
  62.3 0.7 %copy.17 = bf16[1,1,128,1024]{3,2,1,0:T(8,128)(2,1)} copy(bf16[1,1,128,1024]{3,2,1,0:T(8,128)(2,1)S(1)} %bitcast.7) | data formatting | bytes 524288
Async XLA Ops:
  1.3 1.0 %copy-start = (bf16[1,1,128,1024]{3,2,1,0:T(8,128)(2,1)S(1)}, bf16[1,1,128,1024]{3,2,1,0:T(8,128)(2,1)}, u32[]{:S(2)}) copy-start(bf16[1,1,128,1024]{3,2,1,0:T(8,128)(2,1)} %param.8) | copy-start | bytes 786436
  2.2 0.9 %copy-start.1 = (bf16[1,64,1024]{2,1,0:T(8,128)(2,1)S(1)}, bf16[1,64,1024]{2,1,0:T(8,128)(2,1)}, u32[]{:S(2)}) copy-start(bf16[1,64,1024]{2,1,0:T(8,128)(2,1)} %param.14) | copy-start | bytes 393220
  3.1 0.7 %copy-start.2 = (bf16[2,1024]{1,0:T(2,128)(2,1)S(1)}, bf16[2,1024]{1,0:T(2,128)(2,1)}, u32[]{:S(2)}) copy-start(bf16[2,1024]{1,0:T(2,128)(2,1)} %head_ref.1) | copy-start | bytes 12292
  3.8 0.7 %copy-start.3 = (s32[1,128]{1,0:T(1,128)S(1)}, s32[1,128]{1,0:T(1,128)}, u32[]{:S(2)}) copy-start(s32[1,128]{1,0:T(1,128)} %id_ref.1) | copy-start | bytes 1540
  4.5 0.7 %copy-start.4 = (s32[1,128]{1,0:T(1,128)S(1)}, s32[1,128]{1,0:T(1,128)}, u32[]{:S(2)}) copy-start(s32[1,128]{1,0:T(1,128)} %click_ref.1) | copy-start | bytes 1540
  5.1 0.7 %copy-start.5 = (s32[1,128]{1,0:T(1,128)S(1)}, s32[1,128]{1,0:T(1,128)}, u32[]{:S(2)}) copy-start(s32[1,128]{1,0:T(1,128)} %convert_ref.1) | copy-start | bytes 1540

commit v6 on v4

--- a/solution.py
+++ b/solution.py
@@ -185,6 +185,13 @@
     @pl.when(section < sections - 1)
     def _():
         send_taps()
+        conv_ref[...] = jnp.zeros_like(conv_ref)
+        type_ref[...] = jnp.zeros_like(type_ref)
+
+    def share_out(user):
+        @pl.loop(1, shards)
+        def _(j):
+            seq_copy(user, seq, lax.rem(seq + j, shards)).start()
 
     mine = pl.ds(pl.multiple_of(me * rows, rows), rows)
 
@@ -275,6 +282,7 @@
         if c > 0:
             later_taps(c - 1)
     later_taps(chunks - 1)
+    share_out(dp)
     x = x_ref[...].astype(f32)
     inv = lax.rsqrt(jnp.mean(x * x, axis=-1, keepdims=True) + EPS)
     normed = x * inv
@@ -295,15 +303,9 @@
     @pl.when(is_last)
     def _():
         send_taps()
-
-    def share_out(user):
-        @pl.loop(1, shards)
-        def _(j):
-            seq_copy(user, seq, lax.rem(seq + j, shards)).start()
-
-    share_out(dp)
-    conv_ref[...] = jnp.zeros_like(conv_ref)
-    type_ref[...] = jnp.zeros_like(type_ref)
+        conv_ref[...] = jnp.zeros_like(conv_ref)
+        type_ref[...] = jnp.zeros_like(type_ref)
+
 
     @pl.loop(1, group)
     def _(i):

time: 62.7 us -> 63.2 us (level)
  no operation moved by 1% of the time
where the time goes in v6:
time: 63.2 us; the launch traced here: 63 us
  Pallas kernels  57.6 us (91%)
  local copies, waits for them, and re-layouts  4.1 us (6%)
  between operations  1.3 us (2%)
    pallas_call x1, Pallas kernels, on_device(): pl.pallas_call(functools.partial(kernel, users, shards, sections, kind_sh...  57.6 us
    unnamed x7, local copies, waits for them, and re-layouts  4.1 us

profile of v6, /device:TPU:0, one launch (start us, length us, event | category | flops | bytes accessed | tf_op | source)
XLA Modules:
  0.0 63.0 jit_solution(8476380226440738931)
XLA Ops:
  1.3 57.6 %shard_map.103 = (f32[384,1024]{1,0:T(8,128)}, f32[8,1024]{1,0:T(8,128)}, bf16[128,1024]{1,0:T(8,128)(2,1)}) custom-call(bf16[128,1024]{1,0:T(8,128)(2,1)} %bitcast.9, s32[1,128]{1,0:T(1,128)} %id_ref.1, s32[1,128]{1,0:T(1,128)} %click_ref.1, s32[1,128]{1,0:T(1,128)} %convert_ref.1, s32[1]{0:T(128)S(6)} %copy.14.length_ref, bf16[3072,1024]{1,0:T(8,128)(2,1)} %bitcast.6, ...), custom_call_target="tpu_custom_call" | custom-call | tf_op jit(solution)/shard_map/pallas_call | solution.py:410
  58.9 0.0 copy-start.1
  58.9 0.0 copy-start
  58.9 2.8 %copy.15 = f32[1,384,1024]{2,1,0:T(8,128)} copy(f32[1,384,1024]{2,1,0:T(8,128)} %bitcast.7) | data formatting | bytes 3145728
  61.7 0.0 copy-done.1
  61.7 0.6 copy.16
  62.3 0.0 copy-done
  62.3 0.7 %copy.17 = bf16[1,1,128,1024]{3,2,1,0:T(8,128)(2,1)} copy(bf16[1,1,128,1024]{3,2,1,0:T(8,128)(2,1)S(1)} %bitcast.8) | data formatting | bytes 524288
Async XLA Ops:
  58.9 2.8 %copy-start.1 = (f32[8,1024]{1,0:T(8,128)S(1)}, f32[8,1024]{1,0:T(8,128)}, u32[]{:S(2)}) copy-start(f32[8,1024]{1,0:T(8,128)} %get-tuple-element.7) | copy-start | bytes 98308
  58.9 3.4 %copy-start = (bf16[128,1024]{1,0:T(8,128)(2,1)S(1)}, bf16[128,1024]{1,0:T(8,128)(2,1)}, u32[]{:S(2)}) copy-start(bf16[128,1024]{1,0:T(8,128)(2,1)} %get-tuple-element.8) | copy-start | bytes 786436
